TPU v7x, 32 devices: a whole 2x2x4 slice. The times are simulated.
32 devices in a mesh: seq: 16 (over z, y, x), tp: 2 (over core).
Axes of the slice: x: 2, y: 2, z: 4, core: 2. Of those that a mesh axis runs over, the one named last changes fastest.
Arguments:
- tokens: bfloat16 [16384, 1024], P(('seq', 'tp')), may hold values from -6 to 6
- norm_gain: float32 [1024], replicated, may hold values from 0.5 to 1.5
- query_weight: bfloat16 [1024, 1024], P(None, 'tp'), may hold values from -0.1875 to 0.1875
- key_weight: bfloat16 [1024, 1024], P(None, 'tp'), may hold values from -0.1875 to 0.1875
- value_weight: bfloat16 [1024, 1024], P(None, 'tp'), may hold values from -0.1875 to 0.1875
- forget_weight: bfloat16 [1024, 256], P(None, 'tp'), may hold values from -0.09375 to 0.09375
- forget_bias: float32 [256], P('tp'), may hold values from 1 to 10
- head_gain: float32 [1024], P('tp'), may hold values from 0.5 to 1.5
- out_weight: bfloat16 [1024, 1024], P('tp'), may hold values from -0.1875 to 0.1875
- feed_gain: float32 [1024], replicated, may hold values from 0.5 to 1.5
- gate_weight: bfloat16 [1024, 2816], P(None, 'tp'), may hold values from -0.1875 to 0.1875
- up_weight: bfloat16 [1024, 2816], P(None, 'tp'), may hold values from -0.1875 to 0.1875
- down_weight: bfloat16 [2816, 1024], P('tp'), may hold values from -0.109375 to 0.109375
- lengths: int32 [4], replicated, may hold values from 1 to 15424, as said below
- cotangent: bfloat16 [16384, 1024], P(('seq', 'tp')), may hold values from -6 to 6
Outputs:
- block_out: bfloat16 [16384, 1024], P(('seq', 'tp'))
- tokens_grad: bfloat16 [16384, 1024], P(('seq', 'tp'))
- norm_gain_grad: float32 [1024], replicated
- query_weight_grad: float32 [1024, 1024], P(None, 'tp')
- key_weight_grad: float32 [1024, 1024], P(None, 'tp')
- value_weight_grad: float32 [1024, 1024], P(None, 'tp')
- forget_weight_grad: float32 [1024, 256], P(None, 'tp')
- forget_bias_grad: float32 [256], P('tp')
- head_gain_grad: float32 [1024], P('tp')
- out_weight_grad: float32 [1024, 1024], P('tp')
- feed_gain_grad: float32 [1024], replicated
- gate_weight_grad: float32 [1024, 2816], P(None, 'tp')
- up_weight_grad: float32 [1024, 2816], P(None, 'tp')
- down_weight_grad: float32 [2816, 1024], P('tp')
Inputs may be any that keep to these rules, and one draw needn't show every extreme that they name: `lengths`: every length lies between 64 * (k - 1) + 1 and 64 * k for its bucket count k; the buckets of all 4 sequences fill all 16384 positions exactly; exactly one length is 15424, the others take 1024 - 64 positions of buckets together.
All inputs are finite; a program needn't handle non-finite values.
Results may differ from a plain program's by a relative error of at most 0.023.
Values may be sent and summed in bfloat16 or wider, within the bound.
A program may use at most 192 MiB of HBM per device.

v0:
```python
import jax
import jax.numpy as jnp
from jax import lax
from jax.sharding import PartitionSpec as P

DH = 256
SLOTS = 64
BLK = 64
BUCKET = 64


EPS = 1e-06
NORMALIZER = 8.0
HIGH_PRECISION = lax.Precision.HIGHEST


def entering(value, axis, join, neutral):
    count, mine = (lax.axis_size(axis), lax.axis_index(axis))
    pieces = jax.tree.map(lambda part: lax.all_gather(part, axis), value)
    total = jax.tree.map(
        lambda part, zero: jnp.full_like(part, 0) + jnp.asarray(zero, part.dtype), value, neutral
    )

    def hop(position, total):
        longer = join(total, jax.tree.map(lambda part: part[position], pieces))
        return jax.tree.map(lambda new, old: jnp.where(position < mine, new, old), longer, total)

    return lax.fori_loop(0, count - 1, hop, total)


def entering_2(x, axis, join, neutral):
    count = lax.axis_size(axis)
    place = lax.axis_index(axis)
    ahead = count - 1 - place
    gathered = jax.tree.map(
        lambda a, kind: lax.all_gather(a.astype(kind), axis),
        x,
        jax.tree.map(lambda a: jnp.bfloat16 if a.dtype == jnp.float32 else a.dtype, x),
    )
    state = jax.tree.map(lambda a, e: jnp.zeros_like(a) + jnp.asarray(e, a.dtype), x, neutral)

    def one(hop, state):
        source = count - 1 - hop
        return join(
            state,
            jax.tree.map(
                lambda a, own: lax.dynamic_index_in_dim(a, source, 0, False).astype(own.dtype),
                gathered,
                x,
            ),
        )

    return lax.fori_loop(0, ahead, one, state)


def rms_norm(value, gain):
    return value * lax.rsqrt(jnp.mean(value * value, axis=-1, keepdims=True) + EPS) * gain


def against(left, weight):
    return lax.dot_general(
        left, weight, (((1,), (1,)), ((), ())), preferred_element_type=jnp.float32
    )


def across(left, right):
    return lax.dot_general(
        left, right, (((0,), (0,)), ((), ())), preferred_element_type=jnp.float32
    )


def token_marks(lengths, positions):
    buckets = (lengths + BUCKET - 1) // BUCKET
    spans = buckets * BUCKET
    starts = jnp.cumsum(spans) - spans
    member = (positions[:, None] >= starts[None, :]).astype(jnp.int32)
    segment = jnp.sum(member, axis=1) - 1
    picked = (segment[:, None] == jnp.arange(lengths.shape[0], dtype=jnp.int32)[None, :]).astype(
        jnp.int32
    )
    begin = jnp.sum(picked * starts[None, :], axis=1)
    length = jnp.sum(picked * lengths[None, :], axis=1)
    offset = positions - begin
    return (segment, offset < length, offset == 0)


def slot_weights(gate_log, keep, reset):
    return jnp.where(reset[:, None, None], 1.0, 1.0 - jnp.exp(gate_log)) * keep[:, None, None]


def mixer_block(carry, block):
    key_slot_state, value_slot_state, last_seg = carry
    query_rows, key_rows, value_rows, gate_log, weight, segment = block
    width = query_rows.shape[-1]
    cum = jnp.cumsum(gate_log, axis=0)
    order = jnp.arange(segment.shape[0], dtype=jnp.int32)
    same = (segment[:, None] == segment[None, :]) & (order[:, None] >= order[None, :])
    mask = same[:, :, None, None]
    decay = jnp.where(mask, jnp.exp(jnp.where(mask, cum[:, None] - cum[None, :], 0.0)), 0.0)
    mixed = decay * weight[None]
    decay_factor = jnp.where((segment == last_seg)[:, None, None], jnp.exp(cum), 0.0)
    scores = jnp.einsum("thd,jhd->htj", query_rows, key_rows, precision=HIGH_PRECISION)
    inner = jnp.einsum("htj,tjhm->thm", scores, mixed, precision=HIGH_PRECISION)
    outer_product = decay_factor * jnp.einsum(
        "zuw,ulw->zul", query_rows, key_slot_state, precision=HIGH_PRECISION
    )
    slot_probabilities = jax.nn.softmax((inner + outer_product) * width ** (-0.5), axis=-1)
    reading = jnp.einsum("thm,tjhm->htj", slot_probabilities, mixed, precision=HIGH_PRECISION)
    output_rows = jnp.einsum(
        "isr,srw->isw",
        slot_probabilities * decay_factor,
        value_slot_state,
        precision=HIGH_PRECISION,
    )
    output_rows = output_rows + jnp.einsum(
        "htj,jhd->thd", reading, value_rows, precision=HIGH_PRECISION
    )
    trailing_part = mixed[-1]
    key_following = decay_factor[-1][:, :, None] * key_slot_state + jnp.einsum(
        "lqo,lqi->qoi", trailing_part, key_rows, precision=HIGH_PRECISION
    )
    value_following = decay_factor[-1][:, :, None] * value_slot_state + jnp.einsum(
        "lqo,lqi->qoi", trailing_part, value_rows, precision=HIGH_PRECISION
    )
    return ((key_following, value_following, segment[-1]), output_rows)


def run_mixer(
    query_rows, key_rows, value_rows, gate_log, key_init, value_init, segment, keep, reset, last_seg
):
    weight = slot_weights(gate_log, keep, reset)
    count = query_rows.shape[0] // BLK

    def split(array):
        return array.reshape((count, BLK) + array.shape[1:])

    carry = (key_init, value_init, last_seg)
    blocks = (
        split(query_rows),
        split(key_rows),
        split(value_rows),
        split(gate_log),
        split(weight),
        split(segment),
    )
    _, output_rows = lax.scan(jax.checkpoint(mixer_block), carry, blocks)
    return output_rows.reshape(query_rows.shape)


def run_end(key_rows, value_rows, gate_log, segment, keep, reset, last_seg):
    weight = slot_weights(gate_log, keep, reset)
    cum = jnp.cumsum(gate_log, axis=0)
    total = cum[-1]
    tied = (segment == segment[-1])[:, None, None]
    trailing_part = jnp.where(tied, jnp.exp(jnp.where(tied, total[None] - cum, 0.0)), 0.0) * weight
    fade = jnp.where(segment[-1] == last_seg, jnp.exp(total), 0.0)
    key_within_span = jnp.einsum("lqo,lqi->qoi", trailing_part, key_rows, precision=HIGH_PRECISION)
    value_within_span = jnp.einsum(
        "lqo,lqi->qoi", trailing_part, value_rows, precision=HIGH_PRECISION
    )
    return (fade, key_within_span, value_within_span)


def combine_states(earlier, later):
    fade_early, key_early, value_early = earlier
    fade_late, key_late, value_late = later
    return (
        fade_early * fade_late,
        fade_late[:, :, None] * key_early + key_late,
        fade_late[:, :, None] * value_early + value_late,
    )


def per_device(
    tokens,
    norm_gain,
    query_weight,
    key_weight,
    value_weight,
    forget_weight,
    forget_bias,
    head_gain,
    out_weight,
    feed_gain,
    gate_weight,
    up_weight,
    down_weight,
    lengths,
    cotangent,
):
    own = tokens.astype(jnp.float32)
    normed_own, first_back = jax.vjp(rms_norm, own, norm_gain)
    normed_in, cot_full = (
        lax.all_gather(normed_own.astype(jnp.bfloat16), "tp", axis=0, tiled=True),
        lax.all_gather(cotangent, "tp", axis=0, tiled=True),
    )
    span = normed_in.shape[0]
    start = lax.axis_index("seq") * span
    positions = start + jnp.arange(span, dtype=jnp.int32)
    segment, valid, reset = token_marks(lengths, positions)
    keep = valid.astype(jnp.float32)
    last_seg = token_marks(lengths, jnp.reshape(start - 1, (1,)))[0][0]
    q_raw = jnp.dot(normed_in, query_weight, preferred_element_type=jnp.float32)
    k_raw = jnp.dot(normed_in, key_weight, preferred_element_type=jnp.float32)
    v_raw = jnp.dot(normed_in, value_weight, preferred_element_type=jnp.float32)
    z_raw = jnp.dot(normed_in, forget_weight, preferred_element_type=jnp.float32) + forget_bias
    heads = q_raw.shape[1] // DH

    def features(q_in, k_in, z_in):
        gate_in = jnp.where(valid[:, None], jax.nn.log_sigmoid(z_in) / NORMALIZER, 0.0)
        return (jax.nn.silu(q_in), jax.nn.silu(k_in), gate_in)

    (q_act, k_act, gate_flat), feature_back = jax.vjp(features, q_raw, k_raw, z_raw)
    query_low = q_act.astype(jnp.bfloat16)
    keys_low = k_act.astype(jnp.bfloat16)
    values_low = v_raw.astype(jnp.bfloat16)
    query32 = query_low.astype(jnp.float32).reshape(span, heads, DH)
    keys32 = keys_low.astype(jnp.float32).reshape(span, heads, DH)
    values32 = values_low.astype(jnp.float32).reshape(span, heads, DH)
    gate_log = gate_flat.reshape(span, heads, SLOTS)

    def end_part(keys_in, values_in, gate_in):
        return run_end(keys_in, values_in, gate_in, segment, keep, reset, last_seg)

    (fade, key_within_span, value_within_span), end_back = jax.vjp(
        end_part, keys32, values32, gate_log
    )
    identity = (
        jnp.ones_like(fade),
        jnp.zeros_like(key_within_span),
        jnp.zeros_like(value_within_span),
    )
    _, key_init, value_init = entering(
        (fade, key_within_span, value_within_span), "seq", combine_states, identity
    )

    def mixer_fn(query_in, keys_in, values_in, gate_in, key_start, value_start):
        return run_mixer(
            query_in,
            keys_in,
            values_in,
            gate_in,
            key_start,
            value_start,
            segment,
            keep,
            reset,
            last_seg,
        )

    mixed_out = mixer_fn(query32, keys32, values32, gate_log, key_init, value_init)

    def head_norm(mixed_in, gain_in):
        scaled = rms_norm(mixed_in, gain_in.reshape(heads, DH)) * keep[:, None, None]
        return scaled.reshape(span, heads * DH)

    normed_heads, head_back = jax.vjp(head_norm, mixed_out, head_gain)
    heads_low = normed_heads.astype(jnp.bfloat16)
    attn = lax.psum_scatter(
        jnp.dot(heads_low, out_weight, preferred_element_type=jnp.float32).astype(jnp.bfloat16),
        "tp",
        scatter_dimension=0,
        tiled=True,
    ).astype(jnp.float32)
    resid = own + attn
    hidden_own, second_back = jax.vjp(rms_norm, resid, feed_gain)
    hidden_in = lax.all_gather(hidden_own.astype(jnp.bfloat16), "tp", axis=0, tiled=True)
    gate = jnp.dot(hidden_in, gate_weight, preferred_element_type=jnp.float32)
    upper = jnp.dot(hidden_in, up_weight, preferred_element_type=jnp.float32)

    def swiglu(gate_in, upper_in):
        return jax.nn.silu(gate_in) * upper_in

    act, swiglu_back = jax.vjp(swiglu, gate, upper)
    act_low = act.astype(jnp.bfloat16)
    feed = lax.psum_scatter(
        jnp.dot(act_low, down_weight, preferred_element_type=jnp.float32).astype(jnp.bfloat16),
        "tp",
        scatter_dimension=0,
        tiled=True,
    ).astype(jnp.float32)
    block_out = (resid + feed).astype(jnp.bfloat16)
    down_grad = across(act_low, cot_full)
    act_grad = against(cot_full, down_weight)
    gate_grad32, upper_grad32 = swiglu_back(act_grad)
    gate_grad = gate_grad32.astype(jnp.bfloat16)
    upper_grad = upper_grad32.astype(jnp.bfloat16)
    gate_weight_grad = across(hidden_in, gate_grad)
    up_weight_grad = across(hidden_in, upper_grad)
    hidden_part = against(gate_grad, gate_weight) + against(upper_grad, up_weight)
    hidden_grad = lax.psum_scatter(
        hidden_part.astype(jnp.bfloat16), "tp", scatter_dimension=0, tiled=True
    ).astype(jnp.float32)
    resid_norm_grad, feed_gain_part = second_back(hidden_grad)
    resid_grad = cotangent.astype(jnp.float32) + resid_norm_grad
    attn_grad = lax.all_gather(resid_grad.astype(jnp.bfloat16), "tp", axis=0, tiled=True)
    out_weight_grad = across(heads_low, attn_grad)
    heads_grad = against(attn_grad, out_weight)
    mixed_grad, head_gain_grad = head_back(heads_grad)
    _, mixer_again = jax.vjp(mixer_fn, query32, keys32, values32, gate_log, key_init, value_init)
    query_grad, keys_grad, values_grad, gate_grad_log, key_start_grad, value_start_grad = (
        mixer_again(mixed_grad)
    )
    _, key_end_grad, value_end_grad = entering_2(
        (fade, key_start_grad, value_start_grad), "seq", combine_states, identity
    )
    fade_grad = jnp.sum(key_end_grad * key_init + value_end_grad * value_init, axis=-1)
    more_keys, more_values, more_gate = end_back((fade_grad, key_end_grad, value_end_grad))
    keys_grad = keys_grad + more_keys
    values_grad = values_grad + more_values
    gate_grad_log = gate_grad_log + more_gate
    q_grad32, k_grad32, z_grad32 = feature_back(
        (
            query_grad.reshape(span, heads * DH),
            keys_grad.reshape(span, heads * DH),
            gate_grad_log.reshape(span, heads * SLOTS),
        )
    )
    q_grad = q_grad32.astype(jnp.bfloat16)
    k_grad = k_grad32.astype(jnp.bfloat16)
    v_grad = values_grad.reshape(span, heads * DH).astype(jnp.bfloat16)
    z_grad = z_grad32.astype(jnp.bfloat16)
    query_weight_grad = across(normed_in, q_grad)
    key_weight_grad = across(normed_in, k_grad)
    value_weight_grad = across(normed_in, v_grad)
    forget_weight_grad = across(normed_in, z_grad)
    forget_bias_grad = jnp.sum(z_grad.astype(jnp.float32), axis=0)
    input_part = (
        against(q_grad, query_weight)
        + against(k_grad, key_weight)
        + against(v_grad, value_weight)
        + against(z_grad, forget_weight)
    )
    input_grad = lax.psum_scatter(
        input_part.astype(jnp.bfloat16), "tp", scatter_dimension=0, tiled=True
    ).astype(jnp.float32)
    own_grad, norm_gain_part = first_back(input_grad)
    tokens_grad = (resid_grad + own_grad).astype(jnp.bfloat16)
    summed = lax.psum(
        (
            query_weight_grad,
            key_weight_grad,
            value_weight_grad,
            forget_weight_grad,
            forget_bias_grad,
            head_gain_grad,
            out_weight_grad,
            gate_weight_grad,
            up_weight_grad,
            down_grad,
        ),
        "seq",
    )
    norm_gain_grad, feed_gain_grad = lax.psum((norm_gain_part, feed_gain_part), ("seq", "tp"))
    return (
        block_out,
        tokens_grad,
        norm_gain_grad,
        summed[0],
        summed[1],
        summed[2],
        summed[3],
        summed[4],
        summed[5],
        summed[6],
        feed_gain_grad,
        summed[7],
        summed[8],
        summed[9],
    )


def solution(mesh):
    return jax.shard_map(
        per_device,
        mesh=mesh,
        in_specs=(
            P(("seq", "tp"), None),
            P(),
            P(None, "tp"),
            P(None, "tp"),
            P(None, "tp"),
            P(None, "tp"),
            P("tp"),
            P("tp"),
            P("tp", None),
            P(),
            P(None, "tp"),
            P(None, "tp"),
            P("tp", None),
            P(),
            P(("seq", "tp"), None),
        ),
        out_specs=(
            P(("seq", "tp"), None),
            P(("seq", "tp"), None),
            P(),
            P(None, "tp"),
            P(None, "tp"),
            P(None, "tp"),
            P(None, "tp"),
            P("tp"),
            P("tp"),
            P("tp", None),
            P(),
            P(None, "tp"),
            P(None, "tp"),
            P("tp", None),
        ),
        check_vma=False,
    )
```

profile of v0, /device:TPU:0, one launch (start us, length us, event | category | flops | bytes accessed | tf_op | source)
XLA Modules:
  0.0 3660.4 jit_solution(14708551942258182950)
XLA Ops:
  16.3 9.7 all-gather.13.cloned.1.call-done
  30.5 67.2 %reduce-window.30 = f32[64,2,8,128]{3,2,1,0:T(8,128)} reduce-window(f32[64,2,8,128]{3,2,1,0:T(8,128)} %copy.368, f32[]{:T(128)} %constant.293.clone.1), window={size=1x1x1x128 pad=0_0x0_0x0_0x127_0}, to_apply=%region_6.7 | reduce-window | flops 16646144 | bytes 1048580 | tf_op jit(solution)/shard_map/reduce-window.1
  108.0 8.4 fusion.185
  174.4 40.9 %all_gather.45 = f32[16,2,64]{2,1,0:T(2,128)S(1)} all-gather(f32[1,2,64]{2,1,0:T(2,128)S(1)} %get-tuple-element.1385), channel_id=1, replica_groups=mesh['seq'=16,'tp'=2] {'seq'}, dimensions={0}, use_global_device_ids=true | all-gather | bytes 8704 | tf_op jit(solution)/shard_map/all_gather | solution.py:19
  215.2 34.4 all-gather.23.cloned.1.call-done
  249.7 16.6 while.101
  268.0 441.2 %while.98 = (s32[]{:T(128)}, f32[2,64,256]{2,1,0:T(8,128)S(1)}, f32[2,64,256]{2,1,0:T(8,128)S(1)}, s32[]{:T(128)}, f32[16,64,2,256]{3,1,2,0:T(8,128)}, /*index=5...) while((s32[]{:T(128)}, f32[2,64,256]{2,1,0:T(8,128)S(1)}, ...), condition=%wide.region_14.15_spmd, body=%wide.region_10.14_spmd.sunk | while | flops 170635392 | bytes 5727809 | solution.py:146
  272.1 7.0 fusion.411
  299.6 7.0 fusion.411
  327.1 7.0 fusion.411
  354.6 7.0 fusion.411
  382.2 7.0 fusion.411
  409.7 7.0 fusion.411
  437.3 7.0 fusion.411
  464.8 7.0 fusion.411
  492.3 7.0 fusion.411
  519.8 7.0 fusion.411
  547.4 7.0 fusion.411
  574.9 7.0 fusion.411
  602.4 7.0 fusion.411
  629.9 7.0 fusion.411
  657.5 7.0 fusion.411
  685.0 7.0 fusion.411
  724.8 8.3 reduce-scatter.5.cloned.1.call-done
  737.3 11.3 all-gather.15.cloned.1.call-done
  748.6 8.5 fusion.204
  762.4 10.3 multiply_convert_fusion
  782.2 10.0 reduce-scatter.9.cloned.1.call-done
  799.0 152.2 %while.100 = (s32[]{:T(128)}, f32[2,64,256]{2,1,0:T(8,128)S(1)}, f32[2,64,256]{2,1,0:T(8,128)S(1)}, s32[]{:T(128)}, f32[16,2,64,256]{3,2,1,0:T(8,128)}, /*index=...) while((s32[]{:T(128)}, f32[2,64,256]{2,1,0:T(8,128)S(1)}, ...), condition=%wide.region_24.25_spmd.clone, body=%wide.region_22.24_spmd.clone.sunk | while | flops 51056832 | bytes 1682152 | solution.py:146
  973.5 1425.4 %while.102 = (s32[]{:T(128)}, f32[2,64,256]{2,1,0:T(8,128)}, f32[2,64,256]{2,1,0:T(8,128)}, f32[16,64,2,256]{3,1,2,0:T(8,128)}, f32[16,64,2,256]{3,1,0,2:T(8,128...) while((s32[]{:T(128)}, f32[2,64,256]{2,1,0:T(8,128)}, ...), condition=%wide.region_36.37_spmd.clone, body=%wide.region_25.36_spmd.clone.sunk | while | flops 383504192 | bytes 14096787 | solution.py:146
  1016.8 8.2 fusion.473
  1105.9 8.2 fusion.473
  1195.0 8.2 fusion.473
  1284.1 8.2 fusion.473
  1373.2 8.2 fusion.473
  1462.3 8.2 fusion.473
  1551.5 8.2 fusion.473
  1624.7 6.1 fusion.464
  1640.6 8.2 fusion.473
  1713.8 6.1 fusion.464
  1729.7 8.2 fusion.473
  1802.9 6.1 fusion.464
  1818.8 8.2 fusion.473
  1892.1 6.1 fusion.464
  1907.9 8.2 fusion.473
  1981.2 6.1 fusion.464
  1997.0 8.2 fusion.473
  2070.3 6.1 fusion.464
  2086.1 8.2 fusion.473
  2159.4 6.1 fusion.464
  2175.2 8.2 fusion.473
  2264.4 8.2 fusion.473
  2353.5 8.2 fusion.473
  2402.1 40.9 %all_gather.53 = bf16[16,2,64]{2,1,0:T(2,128)(2,1)S(1)} all-gather(bf16[1,2,64]{2,1,0:T(2,128)(2,1)} %get-tuple-element.1384), channel_id=1, replica_groups=mesh['seq'=16,'tp'=2] {'seq'}, dimensions={0}, use_global_device_ids=true | all-gather | bytes 4352 | tf_op jit(solution)/shard_map/all_gather | solution.py:36
  2466.0 47.8 %all-gather.27.cloned.1.call-done = bf16[32,64,256]{2,1,0:T(8,128)(2,1)} async-done(((bf16[2,64,256]{2,1,0:T(8,128)(2,1)}), bf16[32,64,256]{2,1,0:T(8,128)(2,1)}) %all-gather.27.cloned.1.call-update) | async-done | bytes 1048592 | tf_op jit(solution)/shard_map/all_gather | solution.py:36
  2513.8 15.6 while.99
  2538.2 7.7 fusion.190
  2550.4 158.9 %reduce-window.32 = f32[64,2,8,128]{3,2,1,0:T(8,128)S(1)} reduce-window(f32[64,2,8,128]{3,2,1,0:T(8,128)} %copy.419, f32[]{:T(128)} %constant.293.clone.1), window={size=1x1x1x128 pad=0_0x0_0x0_0x0_127}, to_apply=%region_41.42 | reduce-window | flops 16646144 | bytes 1048580 | tf_op jit(solution)/shard_map/reduce-window.3
  2715.9 11.5 fusion.158
  2743.9 6.4 convolution_convert_fusion
  2750.6 8.6 fusion.219
  2782.4 39.8 %all-reduce.5 = (f32[128]{0:T(128)}, f32[512]{0:T(512)}) all-reduce(f32[128]{0:T(128)S(1)} %get-tuple-element.1380, f32[512]{0:T(512)S(1)} %bitcast.762), channel_id=1, replica_groups=mesh['seq'=16,'tp'=2] {'seq'}, use_global_device_ids=true, to_apply=%region_52.53 | all-reduce | flops 640 | bytes 5120 | tf_op jit(solution)/shard_map/psum | solution.py:339
  2824.7 41.2 %all-reduce.4 = (f32[1024]{0:T(1024)}, f32[1024]{0:T(1024)}) all-reduce(f32[1024]{0:T(1024)S(1)} %get-tuple-element.1247, f32[1024]{0:T(1024)S(1)} %copy-done.71), channel_id=1, replica_groups=mesh['seq'=16,'tp'=2] {'seq','tp'}, use_global_device_ids=true, to_apply=%region_46.47 | all-reduce | flops 2048 | bytes 16384 | tf_op jit(solution)/shard_map/psum | solution.py:354
  2870.6 761.5 %all-reduce.9.cloned.1.call-done = (f32[1024,512]{1,0:T(8,128)}, f32[1024,512]{1,0:T(8,128)}, f32[1024,512]{1,0:T(8,128)}, f32[1024,128]{1,0:T(8,128)}, f32[512,...) async-done(((f32[1024,512]{1,0:T(8,128)}, f32[1024,512]{1,0:T(8,128)}, f32[1024,512]{1,0:T(8,128)}, f32[1024,128]{1,0:T(8,128)}, ...) | async-done | bytes 26214416 | tf_op jit(solution)/shard_map/psum | solution.py:339
  (2100 shorter events, 1996.4 us)
Async XLA Ops:
  7.2 755.3 %copy-start = (bf16[1408,1024]{1,0:T(8,128)(2,1)S(1)}, bf16[1408,1024]{1,0:T(8,128)(2,1)}, u32[]{:S(2)}) copy-start(bf16[1408,1024]{1,0:T(8,128)(2,1)} %param.37) | copy-start | bytes 8650756
  7.2 18.9 copy-start.86
  7.2 18.8 all-gather.13.cloned.1.call-start
  12.6 202.6 %all-gather.21.cloned.1.call-start = ((), (), s32[]{:S(2)}) async-start(), calls=%async_computation.12 | async-start | bytes 2228224 | tf_op jit(solution)/shard_map/all_gather | solution.py:19
  16.3 91.8 %copy-start.65 = (pred[1024]{0:T(1024)(128)(4,1)}, pred[1024]{0:T(1024)(128)(4,1)S(1)}, u32[]{:S(2)}) copy-start(pred[1024]{0:T(1024)(128)(4,1)S(1)} %broadcast_compare_fusion.4) | copy-start | bytes 3076
  16.3 13.3 copy-start.74
  16.3 91.7 %copy-start.50 = (f32[1024]{0:T(1024)}, f32[1024]{0:T(1024)S(1)}, u32[]{:S(2)}) copy-start(f32[1024]{0:T(1024)S(1)} %get-tuple-element.1386) | copy-start | bytes 12292
  16.3 91.7 %copy-start.69 = (pred[1024]{0:T(1024)(128)(4,1)}, pred[1024]{0:T(1024)(128)(4,1)S(1)}, u32[]{:S(2)}) copy-start(pred[1024]{0:T(1024)(128)(4,1)S(1)} %get-tuple-element.1424) | copy-start | bytes 3076
  29.5 76.1 %copy-start.29 = (f32[1024,128]{0,1:T(8,128)}, f32[1024,128]{0,1:T(8,128)S(1)}, u32[]{:S(2)}) copy-start(f32[1024,128]{0,1:T(8,128)S(1)} %get-tuple-element.1425) | copy-start | bytes 1572868
  125.5 124.2 %all-gather.23.cloned.1.call-start = ((), (), s32[]{:S(2)}) async-start(), calls=%async_computation.13 | async-start | bytes 2228224 | tf_op jit(solution)/shard_map/all_gather | solution.py:19
  131.5 601.6 %reduce-scatter.5.cloned.1.call-start = ((), (), s32[]{:S(2)}) async-start(), calls=%async_computation.5 | async-start | bytes 3145728 | tf_op jit(solution)/shard_map/reduce_scatter | solution.py:259
  132.6 15.4 copy-start.48
  266.3 515.1 %copy-start.18 = (f32[2,64,256]{2,1,0:T(8,128)}, f32[2,64,256]{2,1,0:T(8,128)S(1)}, u32[]{:S(2)}) copy-start(f32[2,64,256]{2,1,0:T(8,128)S(1)} %get-tuple-element.1934) | copy-start | bytes 393220
  724.7 23.8 all-gather.15.cloned.1.call-start
  735.3 60.6 %copy-start.55 = (f32[512]{0:T(512)}, f32[512]{0:T(512)S(1)}, u32[]{:S(2)}) copy-start(f32[512]{0:T(512)S(1)} %fusion.182) | copy-start | bytes 6148
  736.7 25.8 all-gather.17.cloned.1.call-start
  737.2 55.0 %reduce-scatter.9.cloned.1.call-start = ((), (), s32[]{:S(2)}) async-start(), calls=%async_computation.9 | async-start | bytes 3145728 | tf_op jit(solution)/shard_map/reduce_scatter | solution.py:291
  781.3 169.9 %all-gather.19.cloned.1.call-start = ((), (), s32[]{:S(2)}) async-start(), calls=%async_computation.10 | async-start | bytes 3145728 | tf_op jit(solution)/shard_map/all_gather | solution.py:296
  798.9 1667.1 %all-gather.25.cloned.1.call-start = ((), (), s32[]{:S(2)}) async-start(), calls=%async_computation.14 | async-start | bytes 1114112 | tf_op jit(solution)/shard_map/all_gather | solution.py:36
  799.0 152.2 %copy-start.47 = (f32[16,64,2]{1,0,2:T(8,128)S(1)}, f32[16,64,2]{1,0,2:T(8,128)}, u32[]{:S(2)}) copy-start(f32[16,64,2]{1,0,2:T(8,128)} %fusion.179) | copy-start | bytes 24580
  976.5 17.1 copy-start.3
  985.9 10.8 copy-start.57
  1064.7 18.1 copy-start.3
  1075.0 10.8 copy-start.57
  1153.8 18.1 copy-start.3
  1164.1 10.8 copy-start.57
  1242.9 18.1 copy-start.3
  1253.2 10.8 copy-start.57
  1332.0 18.1 copy-start.3
  1342.4 10.8 copy-start.57
  1421.2 18.1 copy-start.3
  1431.5 10.8 copy-start.57
  1510.3 18.1 copy-start.3
  1520.6 10.8 copy-start.57
  1599.4 18.1 copy-start.3
  1609.7 10.8 copy-start.57
  1688.5 18.1 copy-start.3
  1698.8 10.8 copy-start.57
  1777.6 18.1 copy-start.3
  1866.7 18.1 copy-start.3
  1955.9 18.1 copy-start.3
  2045.0 18.1 copy-start.3
  2055.3 10.8 copy-start.57
  2134.1 18.1 copy-start.3
  2144.4 10.8 copy-start.57
  2223.2 18.1 copy-start.3
  2233.5 10.8 copy-start.57
  2312.3 18.1 copy-start.3
  2400.5 113.3 %all-gather.27.cloned.1.call-start = ((), (), s32[]{:S(2)}) async-start(), calls=%async_computation.15 | async-start | bytes 1114112 | tf_op jit(solution)/shard_map/all_gather | solution.py:36
  2402.1 420.1 %reduce-scatter.11.cloned.1.call-start = ((), (), s32[]{:S(2)}) async-start(), calls=%async_computation.11 | async-start | bytes 3145728 | tf_op jit(solution)/shard_map/reduce_scatter | solution.py:334
  2513.8 18.4 copy-start.19
  2513.8 18.4 copy-start.22
  2715.9 13.8 copy-start.10
  2743.8 122.1 %reduce-scatter.7.cloned.1.call-start = ((), (), s32[]{:S(2)}) async-start(), calls=%async_computation.7 | async-start | bytes 3145728 | tf_op jit(solution)/shard_map/reduce_scatter | solution.py:276
  2750.3 881.8 %all-reduce.9.cloned.1.call-start = ((), (), s32[]{:S(2)}) async-start(), calls=%async_computation.16 | async-start | bytes 52428800 | tf_op jit(solution)/shard_map/psum | solution.py:339
  2781.7 40.5 %copy-start.58 = (f32[1024]{0:T(1024)S(1)}, f32[1024]{0:T(1024)}, u32[]{:S(2)}) copy-start(f32[1024]{0:T(1024)} %param.26) | copy-start | bytes 12292
  2781.7 40.5 %copy-start.60 = (f32[512]{0:T(512)S(1)}, f32[512]{0:T(512)}, u32[]{:S(2)}) copy-start(f32[512]{0:T(512)} %copy-done.59) | copy-start | bytes 6148
  2781.7 42.9 %copy-start.71 = (f32[1024]{0:T(1024)S(1)}, f32[1024]{0:T(1024)}, u32[]{:S(2)}) copy-start(f32[1024]{0:T(1024)} %get-tuple-element.1245) | copy-start | bytes 12292
  2781.7 84.1 %copy-start.62 = (f32[512]{0:T(512)S(1)}, f32[512]{0:T(512)}, u32[]{:S(2)}) copy-start(f32[512]{0:T(512)} %copy-done.61) | copy-start | bytes 6148
  2781.7 84.2 %copy-start.54 = (f32[1024]{0:T(1024)S(1)}, f32[1024]{0:T(1024)}, u32[]{:S(2)}) copy-start(f32[1024]{0:T(1024)} %param.34) | copy-start | bytes 12292
  2781.8 84.2 %copy-start.56 = (f32[512]{0:T(512)S(1)}, f32[512]{0:T(512)}, u32[]{:S(2)}) copy-start(f32[512]{0:T(512)} %copy-done.55) | copy-start | bytes 6148
  2781.8 84.2 %copy-start.64 = (f32[512]{0:T(512)S(1)}, f32[512]{0:T(512)}, u32[]{:S(2)}) copy-start(f32[512]{0:T(512)} %copy-done.63) | copy-start | bytes 6148
  3632.1 11.8 slice-start.4
  3635.3 11.5 slice-start.2
  (181 other events, 578.8 us)
Sparse Core Ops, SparseCore 0:
  12.7 13.2 all-gather.12
  125.6 61.9 all-gather.20
  190.4 59.1 all-gather.22
  724.8 8.2 reduce-scatter.4
  736.8 11.7 all-gather.14
  750.0 11.7 all-gather.16
  781.5 10.7 reduce-scatter.8
  799.0 11.7 all-gather.18
  2400.6 56.4 all-gather.24
  2459.7 54.0 all-gather.26
  2743.9 5.7 reduce-scatter.10
  2752.5 10.7 reduce-scatter.6
  2781.8 850.2 all-reduce.8
where the time goes:
time: 3710 us; the launch traced here: 3660 us
  matrix products  951 us (26%)
  waiting for transfers between devices  884 us (24%)
  other arithmetic  841 us (23%)
  local copies, waits for them, and re-layouts  776 us (21%)
  blocking collectives  163 us (4%)
    psum x1, waiting for transfers between devices, per_device(): lax.psum((query_weight_grad, key_weight_grad, value_weight_grad, forget_w...  762 us
    another operation x11, other arithmetic  231 us
    dot_general x32, matrix products, mixer_block(): inner = jnp.einsum('htj,tjhm->thm', scores, mixed, precision=HIGH_PRECISION)  206 us
    dot_general x32, matrix products, mixer_block(): jnp.einsum('thm,tjhm->htj', slot_probabilities, mixed, precision=HIGH_PRE...  180 us
    reduce_sum x16, other arithmetic, mixer_block(): cum[:, None] - cum[None, :]  131 us
    squeeze x96, local copies, waits for them, and re-layouts, run_mixer(): _, output_rows = lax.scan(jax.checkpoint(mixer_block), carry, blocks)  128 us
    while x32, other arithmetic  97 us
    another operation x80, other arithmetic, mixer_block(): cum = jnp.cumsum(gate_log, axis=0)  90.3 us
  transfers between devices with their start and end apart: 13, of which 7 were waited for; matrix products, arithmetic and copies ran while one was open for 7% of the time, Pallas kernels for 0%

commit v1 on v0

v1 whole, which is shorter than its diff:
```python
import functools

import jax
import jax.numpy as jnp
import numpy as np
from jax import lax
from jax.experimental import pallas as pl
from jax.experimental.pallas import tpu as pltpu
from jax.sharding import PartitionSpec as P

DH = 256
SLOTS = 64
BUCKET = 64
CH = 128
BASE = 8
HALVES = (64, 32, 16, 8)
RESET_LOG = -16384.0
LIFT = 2.0**20
SCALE = DH**-0.5

EPS = 1e-06
NORMALIZER = 8.0

BF = jnp.bfloat16
F32 = jnp.float32
VMEM_LIMIT = 56 * 1024 * 1024


def dot(a, b):
    return lax.dot_general(a, b, (((1,), (0,)), ((), ())), preferred_element_type=F32)


def nt(a, b):
    return lax.dot_general(a, b, (((1,), (1,)), ((), ())), preferred_element_type=F32)


def tn(a, b):
    return lax.dot_general(a, b, (((0,), (0,)), ((), ())), preferred_element_type=F32)


def tables():
    t, u = np.arange(CH)[:, None], np.arange(CH)[None, :]
    sums, pairs = [u <= t, u > t], []
    for half in HALVES:
        mid = t // (2 * half) * (2 * half) + half
        sums.append(np.where(t >= mid, (u >= mid) & (u <= t), (u > t) & (u < mid)))
        pairs.append(
            (t // (2 * half) == u // (2 * half)) & (t % (2 * half) >= half) & (u % (2 * half) < half)
        )
    ref = t // BASE * BASE + BASE // 2 - 1
    sums.append(((u > ref) & (u <= t)).astype(int) - ((u > t) & (u <= ref)).astype(int))
    pairs.append((t // BASE == u // BASE) & (u <= t))
    stacked = np.concatenate([s.astype(np.float32) for s in sums], 0)
    back = np.concatenate([(u >= t), (u >= t) & ((t >= BUCKET) | (u < BUCKET))], 0).astype(np.float32)
    return (
        np.concatenate([stacked] * 3, 1),
        np.stack(pairs).astype(np.float32),
        np.stack([p.T for p in pairs]).astype(np.float32),
        np.concatenate([back] * 3, 1),
    )


def split3(x):
    high = x.astype(BF)
    rest = x - high.astype(F32)
    middle = rest.astype(BF)
    low = (rest - middle.astype(F32)).astype(BF)
    return jnp.concatenate([high, middle, low], 0)


def decays(gate, weight, sums_ref):
    sums = dot(sums_ref[...], split3(gate))
    part = [sums[i * CH : (i + 1) * CH] for i in range(3 + len(HALVES))]
    first, last = jnp.exp(part[0]), jnp.exp(part[1])
    rows = [jnp.exp(p) for p in part[2:-1]]
    cols = [r * weight for r in rows]
    slopes = list(rows)
    rows.append(jnp.exp(part[-1]) * LIFT)
    slopes.append(jnp.exp(-part[-1]) * (1 / LIFT))
    cols.append(slopes[-1] * weight)
    return first, last, rows, cols, slopes


def halves(x):
    left = lax.broadcasted_iota(jnp.int32, x.shape, 1) < SLOTS
    zero = jnp.zeros_like(x)
    return jnp.where(left, x, zero), jnp.where(left, zero, x)


def head(x, h):
    return x[:, h * DH : (h + 1) * DH]


def slots(x, h):
    return x[:, h * SLOTS : (h + 1) * SLOTS]


def state(x, h):
    return x[h * SLOTS : (h + 1) * SLOTS]


def through(pairwise, rows, cols, pairs_ref):
    total = None
    for i in range(len(rows)):
        keep = pairs_ref[i] != 0
        left = jnp.concatenate([jnp.where(keep, p, 0.0).astype(BF) for p in pairwise], 1)
        right = jnp.concatenate(halves(cols[i].astype(BF)), 0)
        term = rows[i] * dot(left, right)
        total = term if total is None else total + term
    return total


def back_through(values, rows, cols, pairs_ref):
    totals = None
    for i in range(len(rows)):
        keep = pairs_ref[i] != 0
        stack = [part for v in values for part in halves((v * rows[i]).astype(BF))]
        out = nt(jnp.concatenate(stack, 0), cols[i].astype(BF))
        terms = [jnp.where(keep, out[n * CH : (n + 1) * CH], 0.0) for n in range(len(stack))]
        totals = terms if totals is None else [a + b for a, b in zip(totals, terms)]
    return totals


def softmax2(logits):
    out = []
    for h in range(2):
        x = slots(logits, h) * SCALE
        e = jnp.exp(x - jnp.max(x, axis=-1, keepdims=True))
        out.append(e / jnp.sum(e, axis=-1, keepdims=True))
    return jnp.concatenate(out, 1)


def fade_of(gate):
    return jnp.exp(jnp.sum(gate.T, axis=1, keepdims=True))


def run_part(trail, keys, values):
    return jnp.concatenate(
        [
            jnp.concatenate([tn(slots(trail, h), head(keys, h)), tn(slots(trail, h), head(values, h))], 1)
            for h in range(2)
        ],
        0,
    )


def project_kernel(
    tp_ref, own_ref, other_ref, gain_ref, wq_ref, wk_ref, wv_ref, wf_ref, bias_ref, code_ref, sums_ref,
    xn_ref, q_ref, k_ref, v_ref, dsq_ref, dsk_ref, gate_ref, weight_ref, dz_ref, kv_ref, fade_ref,
):
    step = pl.program_id(0)
    mine = step // (pl.num_programs(0) // 2) == tp_ref[0]
    x = jnp.where(mine, own_ref[...], other_ref[...]).astype(F32)
    mean = jnp.mean(x * x, axis=-1, keepdims=True)
    xn = (x * lax.rsqrt(mean + EPS) * gain_ref[...]).astype(BF)
    xn_ref[...] = xn

    def silu(raw):
        s = 1.0 / (1.0 + jnp.exp(-raw))
        return (raw * s).astype(BF), (s * (1.0 + raw * (1.0 - s))).astype(BF)

    q, dsq = silu(dot(xn, wq_ref[...]))
    q_ref[...], dsq_ref[...] = q, dsq
    k, dsk = silu(dot(xn, wk_ref[...]))
    k_ref[...], dsk_ref[...] = k, dsk
    v = dot(xn, wv_ref[...]).astype(BF)
    v_ref[...] = v
    z = dot(xn, wf_ref[...]) + bias_ref[...]
    code = code_ref[...]
    valid, reset = code > 0.5, code > 1.5
    soft = jnp.log(1.0 + jnp.exp(-jnp.abs(z)))
    log_sig = jnp.minimum(z, 0.0) - soft
    gate = jnp.where(valid, log_sig * (1.0 / NORMALIZER), 0.0)
    weight = jnp.where(reset, 1.0, 1.0 - jnp.exp(gate))
    gate = jnp.where(reset, RESET_LOG, gate)
    down = jnp.exp(-jnp.abs(z))
    sig_neg = jnp.where(z > 0, down, 1.0) / (1.0 + down)
    gate_ref[...] = gate
    weight_ref[...] = weight
    dz_ref[...] = jnp.where(valid & (code < 1.5), sig_neg * (1.0 / NORMALIZER), 0.0)
    last = jnp.exp(dot(sums_ref[CH : 2 * CH], split3(gate)))
    part = run_part((last * weight).astype(BF), k, v)
    fade = fade_of(gate)

    @pl.when(step == 0)
    def _():
        kv_ref[...] = part
        fade_ref[...] = jnp.broadcast_to(fade, fade_ref.shape)

    @pl.when(step > 0)
    def _():
        kv_ref[...] = fade * kv_ref[...] + part
        fade_ref[...] = fade_ref[...] * fade


def mix_kernel(
    tp_ref, q_ref, k_ref, v_ref, gate_ref, weight_ref, code_ref, start_ref, sums_ref, pairs_ref, gain_ref, wo_ref,
    logit_ref, kvs_ref, mixed_ref, normed_ref, own_ref, other_ref, kv_ref,
):
    step = pl.program_id(0)

    @pl.when(step == 0)
    def _():
        kv_ref[...] = start_ref[...]

    q, k, v = q_ref[...], k_ref[...], v_ref[...]
    gate, weight = gate_ref[...], weight_ref[...]
    first, last, rows, cols, _ = decays(gate, weight, sums_ref)
    kv = kv_ref[...]
    kvs_ref[0] = kv
    low = kv.astype(BF)
    scores = [nt(head(q, h), head(k, h)) for h in range(2)]
    outer = jnp.concatenate([nt(head(q, h), state(low, h)[:, :DH]) for h in range(2)], 1)
    logits = first * outer + through(scores, rows, cols, pairs_ref)
    logit_ref[...] = logits
    probs = softmax2(logits)
    reading = back_through([probs], rows, cols, pairs_ref)
    spread = (probs * first).astype(BF)
    kv_ref[...] = fade_of(gate) * kv + run_part((last * weight).astype(BF), k, v)
    code = code_ref[:, :1]
    normed = []
    for h in range(2):
        mixed = dot(slots(spread, h), state(low, h)[:, DH:]) + dot(reading[h].astype(BF), head(v, h))
        mixed_ref[:, h * DH : (h + 1) * DH] = mixed
        r = lax.rsqrt(jnp.mean(mixed * mixed, axis=-1, keepdims=True) + EPS)
        r = jnp.where(code > 0.5, r, 0.0)
        normed.append((mixed * r * gain_ref[:, h * DH : (h + 1) * DH]).astype(BF))
    normed = jnp.concatenate(normed, 1)
    normed_ref[...] = normed
    attn = dot(normed, wo_ref[...]).astype(BF)
    mine = step // (pl.num_programs(0) // 2) == tp_ref[0]

    @pl.when(mine)
    def _():
        own_ref[...] = attn

    @pl.when(jnp.logical_not(mine))
    def _():
        other_ref[...] = attn


def score_kernel(
    tp_ref, da_own_ref, da_other_ref, wo_ref, mixed_ref, code_ref, gain_ref, q_ref, k_ref, v_ref, gate_ref, weight_ref,
    logit_ref, kvs_ref, sums_ref, pairs_ref,
    da_ref, dmix_ref, dl_ref, y_ref, gain_grad_ref, dkv_ref, reach_ref,
):
    step = pl.program_id(0)
    mine = step // (pl.num_programs(0) // 2) == tp_ref[0]
    da = jnp.where(mine, da_own_ref[...], da_other_ref[...])
    da_ref[...] = da
    dnormed = nt(da, wo_ref[...])
    dnormed = jnp.where(code_ref[:, :1] > 0.5, dnormed, 0.0)
    dmix, gain_grad = [], []
    for h in range(2):
        mixed = mixed_ref[:, h * DH : (h + 1) * DH]
        r = lax.rsqrt(jnp.mean(mixed * mixed, axis=-1, keepdims=True) + EPS)
        n = mixed * r
        d = head(dnormed, h)
        u = d * gain_ref[:, h * DH : (h + 1) * DH]
        gain_grad.append(jnp.sum(d * n, axis=0, keepdims=True))
        dmix.append((r * (u - n * jnp.mean(u * n, axis=-1, keepdims=True))).astype(BF))
    gain_grad = jnp.concatenate(gain_grad, 1)
    dmix = jnp.concatenate(dmix, 1)
    dmix_ref[...] = dmix
    q, k, v = q_ref[...], k_ref[...], v_ref[...]
    gate, weight = gate_ref[...], weight_ref[...]
    first, _, rows, cols, _ = decays(gate, weight, sums_ref)
    logits = logit_ref[...]
    probs = softmax2(logits)
    low = kvs_ref[0].astype(BF)
    reads = [nt(head(dmix, h), head(v, h)) for h in range(2)]
    outer = jnp.concatenate([nt(head(dmix, h), state(low, h)[:, DH:]) for h in range(2)], 1)
    dprobs = first * outer + through(reads, rows, cols, pairs_ref)
    weighted = probs * dprobs
    sums = [
        jnp.broadcast_to(jnp.sum(slots(weighted, h), axis=-1, keepdims=True), (CH, SLOTS)) for h in range(2)
    ]
    dl = (weighted - probs * jnp.concatenate(sums, 1)) * SCALE
    dl_ref[...] = dl
    y_ref[...] = dl * logits + weighted
    part = state_grads(dl, probs, first, q, dmix)
    fade = fade_of(gate)

    @pl.when(step == 0)
    def _():
        gain_grad_ref[...] = gain_grad
        dkv_ref[...] = part
        reach_ref[...] = jnp.broadcast_to(fade, reach_ref.shape)

    @pl.when(step > 0)
    def _():
        gain_grad_ref[...] += gain_grad
        reach = reach_ref[...]
        dkv_ref[...] += jnp.concatenate([reach] * (dkv_ref.shape[1] // reach.shape[1]), 1) * part
        reach_ref[...] = reach * fade


def state_grads(dl, probs, first, q, dmix):
    a, b = (dl * first).astype(BF), (probs * first).astype(BF)
    return jnp.concatenate(
        [jnp.concatenate([tn(slots(a, h), head(q, h)), tn(slots(b, h), head(dmix, h))], 1) for h in range(2)], 0
    )


def grad_kernel(
    tp_ref, q_ref, k_ref, v_ref, dsq_ref, dsk_ref, gate_ref, weight_ref, dz_ref, logit_ref, kvs_ref, dmix_ref, dl_ref, y_ref,
    end_ref, flow_ref, sums_ref, pairs_ref, flipped_ref, back_ref, wq_ref, wk_ref, wv_ref, wf_ref,
    dq_ref, dk_ref, dv_ref, df_ref, bias_ref, own_ref, other_ref, dkv_ref, carry_ref,
):
    step = pl.program_id(0)

    @pl.when(step == 0)
    def _():
        dkv_ref[...] = end_ref[...]
        carry_ref[...] = flow_ref[...]

    q, k, v, dmix = q_ref[...], k_ref[...], v_ref[...], dmix_ref[...]
    gate, weight = gate_ref[...], weight_ref[...]
    dl = dl_ref[...]
    first, last, rows, cols, slopes = decays(gate, weight, sums_ref)
    probs = softmax2(logit_ref[...])
    kv, dkv = kvs_ref[0], dkv_ref[...]
    low, dlow = kv.astype(BF), dkv.astype(BF)
    r0, r1, s0, s1 = back_through([probs, dl], rows, cols, pairs_ref)
    turned = [
        nt(head(a, h), head(b, h)) for h in range(2) for a, b in ((k, q), (v, dmix))
    ]
    dw = last * jnp.concatenate(
        [nt(jnp.concatenate([head(k, h), head(v, h)], 1), state(dlow, h)) for h in range(2)], 1
    )
    for i in range(len(rows)):
        keep = flipped_ref[i] != 0
        left = jnp.concatenate([jnp.where(keep, x, 0.0).astype(BF) for x in turned], 1)
        a, b = halves((dl * rows[i]).astype(BF)), halves((probs * rows[i]).astype(BF))
        dw = dw + slopes[i] * dot(left, jnp.concatenate([a[0], b[0], a[1], b[1]], 0))
    trail = (last * weight).astype(BF)
    spread = (dl * first).astype(BF)
    reading, dscore = [r0.astype(BF), r1.astype(BF)], [s0.astype(BF), s1.astype(BF)]
    dq, dk, dv = [], [], []
    for h in range(2):
        dq.append(dot(dscore[h], head(k, h)) + dot(slots(spread, h), state(low, h)[:, :DH]))
        dk.append(tn(dscore[h], head(q, h)) + dot(slots(trail, h), state(dlow, h)[:, :DH]))
        dv.append(tn(reading[h], head(dmix, h)) + dot(slots(trail, h), state(dlow, h)[:, DH:]))
    dq = (jnp.concatenate(dq, 1) * dsq_ref[...].astype(F32)).astype(BF)
    dk = (jnp.concatenate(dk, 1) * dsk_ref[...].astype(F32)).astype(BF)
    dv = jnp.concatenate(dv, 1).astype(BF)
    both = dot(back_ref[...], split3(y_ref[...] - weight * dw))
    cut = gate[BUCKET : BUCKET + 1] < 0.5 * RESET_LOG
    late = lax.broadcasted_iota(jnp.int32, gate.shape, 0) >= BUCKET
    flow = jnp.where(cut, both[CH:], both[:CH]) + jnp.where(cut & jnp.logical_not(late), 0.0, carry_ref[...])
    df = ((flow - jnp.exp(gate) * dw) * dz_ref[...]).astype(BF)
    dq_ref[...], dk_ref[...], dv_ref[...], df_ref[...] = dq, dk, dv, df
    bias_part = jnp.sum(df.astype(F32), axis=0, keepdims=True)
    new = fade_of(gate) * dkv + state_grads(dl, probs, first, q, dmix)
    dkv_ref[...] = new
    carry_ref[...] = jnp.sum((kv * new).T, axis=0, keepdims=True)
    dx = (nt(dq, wq_ref[...]) + nt(dk, wk_ref[...]) + nt(dv, wv_ref[...]) + nt(df, wf_ref[...])).astype(BF)
    n = pl.num_programs(0)
    mine = (n - 1 - step) // (n // 2) == tp_ref[0]

    @pl.when(mine)
    def _():
        own_ref[...] = dx

    @pl.when(jnp.logical_not(mine))
    def _():
        other_ref[...] = dx

    @pl.when(step == 0)
    def _():
        bias_ref[...] = bias_part

    @pl.when(step > 0)
    def _():
        bias_ref[...] += bias_part


def call(kernel, count, ins, outs, scratch=(), tp=None, flops=0, moved=0, name=None):
    grid_spec = pltpu.PrefetchScalarGridSpec(
        num_scalar_prefetch=1,
        grid=(count,),
        in_specs=[pl.BlockSpec(block, index) for _, block, index in ins],
        out_specs=[pl.BlockSpec(block, index) for _, _, block, index in outs],
        scratch_shapes=list(scratch),
    )
    return pl.pallas_call(
        kernel,
        grid_spec=grid_spec,
        out_shape=[jax.ShapeDtypeStruct(shape, dtype) for shape, dtype, _, _ in outs],
        compiler_params=pltpu.CompilerParams(
            dimension_semantics=("arbitrary",), vmem_limit_bytes=VMEM_LIMIT
        ),
        cost_estimate=pl.CostEstimate(flops=flops, bytes_accessed=moved, transcendentals=0),
        name=name,
    )(tp, *[a for a, _, _ in ins])


def whole(array):
    return (array, array.shape, lambda i, tp: (0,) * array.ndim)


def rows_of(array):
    return (array, (CH, array.shape[1]), lambda i, tp: (i, 0))


def swap(x):
    return lax.ppermute(x, "tp", [(0, 1), (1, 0)])


def scan_states(total, fade, earlier):
    count = lax.axis_size("seq")
    index = lax.axis_index("seq")
    entering, entering_fade = jnp.zeros_like(total), jnp.ones_like(fade)
    for bit in range(count.bit_length() - 1):
        high = fade.astype(BF)
        sent = jnp.concatenate([total.astype(BF), high, (fade - high.astype(F32)).astype(BF)], 1)
        got = lax.ppermute(sent, "seq", [(i, i ^ (1 << bit)) for i in range(count)])
        width = total.shape[1]
        part = got[:, :width].astype(F32)
        part_fade = got[:, width : width + CH].astype(F32) + got[:, width + CH :].astype(F32)
        behind = ((index >> bit) & 1) == (1 if earlier else 0)
        entering = jnp.where(behind, entering_fade[:, :1] * part + entering, entering)
        entering_fade = jnp.where(behind, entering_fade * part_fade, entering_fade)
        total = jnp.where(behind, fade[:, :1] * part + total, part_fade[:, :1] * total + part)
        fade = fade * part_fade
    return entering


def token_code(lengths, positions):
    buckets = (lengths + BUCKET - 1) // BUCKET
    spans = buckets * BUCKET
    starts = jnp.cumsum(spans) - spans
    segment = jnp.sum((positions[:, None] >= starts[None, :]).astype(jnp.int32), axis=1) - 1
    picked = segment[:, None] == jnp.arange(lengths.shape[0], dtype=jnp.int32)[None, :]
    begin = jnp.sum(jnp.where(picked, starts[None, :], 0), axis=1)
    length = jnp.sum(jnp.where(picked, lengths[None, :], 0), axis=1)
    offset = positions - begin
    return jnp.where(offset == 0, 2.0, jnp.where(offset < length, 1.0, 0.0)).astype(F32)


def row_norm(x, gain):
    r = lax.rsqrt(jnp.mean(x * x, axis=-1, keepdims=True) + EPS)
    return x * r * gain


def row_norm_back(x, gain, grad):
    r = lax.rsqrt(jnp.mean(x * x, axis=-1, keepdims=True) + EPS)
    n = x * r
    u = grad * gain
    return r * (u - n * jnp.mean(u * n, axis=-1, keepdims=True)), jnp.sum(grad * n, axis=0)


def per_device(
    tokens, norm_gain, query_weight, key_weight, value_weight, forget_weight, forget_bias, head_gain,
    out_weight, feed_gain, gate_weight, up_weight, down_weight, lengths, cotangent,
):
    half, width = tokens.shape
    span = 2 * half
    count = span // CH
    cols = query_weight.shape[1]
    lanes = forget_weight.shape[1]
    tp = lax.axis_index("tp").astype(jnp.int32)[None]
    sums, pairs, flipped, back = tables()
    sums, back = jnp.asarray(sums, BF), jnp.asarray(back, BF)
    pairs, flipped = jnp.asarray(pairs), jnp.asarray(flipped)

    tokens_other, cot_other = swap(tokens), swap(cotangent)
    positions = lax.axis_index("seq") * span + jnp.arange(span, dtype=jnp.int32)
    code = jnp.broadcast_to(token_code(lengths, positions)[:, None], (span, lanes))
    half_map = lambda i, tp: (i % (count // 2), 0)
    own_map = lambda i, tp: (jnp.clip(i - tp[0] * (count // 2), 0, count // 2 - 1), 0)
    other_map = lambda i, tp: (jnp.clip(i - (1 - tp[0]) * (count // 2), 0, count // 2 - 1), 0)
    block = (CH, width)
    row = lambda n, d: ((span, n), d, (CH, n), lambda i, tp: (i, 0))
    fixed = lambda shape: (shape, F32, shape, lambda i, tp: (0,) * len(shape))

    xn, q, k, v, dsq, dsk, gate, weight, dzf, kv_run, fade_run = call(
        project_kernel, count,
        [(tokens, block, half_map), (tokens_other, block, half_map), whole(norm_gain[None]), whole(query_weight),
         whole(key_weight), whole(value_weight), whole(forget_weight), whole(forget_bias[None]), rows_of(code), whole(sums)],
        [row(width, BF)] + [row(cols, BF)] * 5 + [row(lanes, F32)] * 3 + [fixed((lanes, 2 * DH)), fixed((lanes, CH))],
        tp=tp, flops=2 * span * width * (3 * cols + lanes), moved=16 << 20, name="project",
    )

    kv_start = scan_states(kv_run, fade_run, True)

    logits, kvs, mixed, normed, attn_own, attn_other = call(
        mix_kernel, count,
        [rows_of(q), rows_of(k), rows_of(v), rows_of(gate), rows_of(weight), rows_of(code), whole(kv_start), whole(sums),
         whole(pairs), whole(head_gain[None]), whole(out_weight)],
        [row(lanes, F32), ((count, lanes, 2 * DH), F32, (1, lanes, 2 * DH), lambda i, tp: (i, 0, 0)), row(cols, F32),
         row(cols, BF), ((half, width), BF, block, own_map), ((half, width), BF, block, other_map)],
        scratch=[pltpu.VMEM((lanes, 2 * DH), F32)],
        tp=tp, flops=4 * span * width * cols, moved=16 << 20, name="mix",
    )

    own = tokens.astype(F32)
    resid = own + (attn_own.astype(F32) + swap(attn_other).astype(F32))
    hidden_own = row_norm(resid, feed_gain).astype(BF)
    hidden = jnp.concatenate([hidden_own, swap(hidden_own)], 0)
    cot = jnp.concatenate([cotangent, cot_other], 0)
    ff_gate = dot(hidden, gate_weight)
    ff_up = dot(hidden, up_weight)
    dact = nt(cot, down_weight)
    sig = jax.nn.sigmoid(ff_gate)
    act = (ff_gate * sig * ff_up).astype(BF)
    dgate = (dact * ff_up * sig * (1.0 + ff_gate * (1.0 - sig))).astype(BF)
    dup = (dact * ff_gate * sig).astype(BF)
    feed = dot(act, down_weight).astype(BF)
    dhidden = (nt(dgate, gate_weight) + nt(dup, up_weight)).astype(BF)
    down_grad = tn(act, cot).astype(BF)
    gate_grad = tn(hidden, dgate).astype(BF)
    up_grad = tn(hidden, dup).astype(BF)
    ff_grads = lax.psum((gate_grad, up_grad, down_grad), "seq")

    dhidden_own = dhidden[:half].astype(F32) + swap(dhidden[half:]).astype(F32)
    block_out = (resid + (feed[:half].astype(F32) + swap(feed[half:]).astype(F32))).astype(BF)
    dresid_norm, feed_gain_part = row_norm_back(resid, feed_gain, dhidden_own)
    dresid = cotangent.astype(F32) + dresid_norm
    da_own = dresid.astype(BF)
    da_other = swap(da_own)

    da, dmix, dl, y, head_gain_grad, dkv_run, reach = call(
        score_kernel, count,
        [(da_own, block, half_map), (da_other, block, half_map), whole(out_weight), rows_of(mixed), rows_of(code),
         whole(head_gain[None]), rows_of(q), rows_of(k), rows_of(v), rows_of(gate), rows_of(weight), rows_of(logits),
         (kvs, (1, lanes, 2 * DH), lambda i, tp: (i, 0, 0)), whole(sums), whole(pairs)],
        [row(width, BF), row(cols, BF), row(lanes, F32), row(lanes, F32), fixed((1, cols)), fixed((lanes, 2 * DH)),
         fixed((lanes, CH))],
        tp=tp, flops=4 * span * width * cols, moved=16 << 20, name="score",
    )

    dkv_end = scan_states(dkv_run, reach, False)
    out_grad = tn(normed, da).astype(BF)
    kv_end = fade_run[:, :1] * kv_start + kv_run
    flow = jnp.sum(kv_end * dkv_end, axis=1)[None]

    turn = lambda i: count - 1 - i
    rows_back = lambda a: (a, (CH, a.shape[1]), lambda i, tp: (turn(i), 0))
    row_back = lambda n, d: ((span, n), d, (CH, n), lambda i, tp: (turn(i), 0))
    dq, dk, dv, df, bias_grad, dx_own, dx_other = call(
        grad_kernel, count,
        [rows_back(a) for a in (q, k, v, dsq, dsk, gate, weight, dzf, logits)]
        + [(kvs, (1, lanes, 2 * DH), lambda i, tp: (turn(i), 0, 0)), rows_back(dmix), rows_back(dl), rows_back(y),
           whole(dkv_end), whole(flow), whole(sums), whole(pairs), whole(flipped), whole(back),
           whole(query_weight), whole(key_weight), whole(value_weight), whole(forget_weight)],
        [row_back(cols, BF)] * 3 + [row_back(lanes, BF), fixed((1, lanes)),
         ((half, width), BF, block, lambda i, tp: own_map(turn(i), tp)),
         ((half, width), BF, block, lambda i, tp: other_map(turn(i), tp))],
        scratch=[pltpu.VMEM((lanes, 2 * DH), F32), pltpu.VMEM((1, lanes), F32)],
        tp=tp, flops=2 * span * width * (3 * cols + lanes), moved=24 << 20, name="grad",
    )

    grads = [tn(xn, d).astype(BF) for d in (dq, dk, dv, df)]
    mixer_grads = lax.psum((*grads, out_grad), "seq")
    dx = dx_own.astype(F32) + swap(dx_other).astype(F32)
    own_grad, norm_gain_part = row_norm_back(own, norm_gain, dx)
    tokens_grad = (dresid + own_grad).astype(BF)
    norm_gain_grad, feed_gain_grad = lax.psum((norm_gain_part, feed_gain_part), ("seq", "tp"))
    bias_sum, head_sum = lax.psum((bias_grad[0], head_gain_grad[0]), "seq")
    wide = [g.astype(F32) for g in (*mixer_grads, *ff_grads)]
    return (
        block_out, tokens_grad, norm_gain_grad, wide[0], wide[1], wide[2], wide[3], bias_sum, head_sum, wide[4],
        feed_gain_grad, wide[5], wide[6], wide[7],
    )


def solution(mesh):
    rows, by_col, by_row = P(("seq", "tp"), None), P(None, "tp"), P("tp", None)
    return jax.shard_map(
        per_device,
        mesh=mesh,
        in_specs=(
            rows, P(), by_col, by_col, by_col, by_col, P("tp"), P("tp"), by_row, P(), by_col, by_col, by_row, P(), rows,
        ),
        out_specs=(
            rows, rows, P(), by_col, by_col, by_col, by_col, P("tp"), P("tp"), by_row, P(), by_col, by_col, by_row,
        ),
        check_vma=False,
    )
```

time: 3710 us -> 639 us (0.17); the launches traced: 3660 us -> 629 us
  matrix products: 951 us -> 64.9 us
  other arithmetic: 841 us -> 52.6 us
  local copies, waits for them, and re-layouts: 776 us -> 10.3 us
  waiting for transfers between devices: 884 us -> 315 us
  blocking collectives: 163 us -> 83.6 us
  Pallas kernels: 0 us -> 70.2 us
    dot_general x446 -> x14, matrix products: 951 us -> 64.9 us  [the longest x8 27.8 us: tn(): lax.dot_general(a, b, (((0,), (0,)), ((), ())), preferred_element_type=F32)]
    psum x1, waiting for transfers between devices: 762 us -> 279 us  [per_device(): mixer_grads = lax.psum((*grads, out_grad), 'seq')]
    another operation x91 -> x2, other arithmetic: 321 us -> 1.12 us
    reduce_sum x76 -> x6, other arithmetic: 205 us -> 7.72 us  [the longest x2 3.53 us: row_norm_back(): jnp.sum(grad * n, axis=0)]
    squeeze x96 -> x0, local copies, waits for them, and re-layouts: 128 us -> none  [run_mixer(): _, output_rows = lax.scan(jax.checkpoint(mixer_block), carry, blocks)]
    dot_general x98 -> x0, local copies, waits for them, and re-layouts: 119 us -> none  [the longest x48 61.3 us: mixer_block(): inner = jnp.einsum('htj,tjhm->thm', scores, mixed, precision=HIGH_PRECISION)]
    all_gather x8 -> x0, waiting for transfers between devices: 103 us -> none  [the longest x2 47.8 us: entering_2(): lax.all_gather(a.astype(kind), axis)]
    while x32 -> x0, other arithmetic: 97 us -> none
  transfers between devices with their start and end apart: 13 -> 17, of which waited for: 7 -> 12; matrix products, arithmetic and copies ran while one was open for 7% -> 7% of each run, Pallas kernels for 0% -> 0%
where the time goes in v1:
time: 639 us; the launch traced here: 629 us
  waiting for transfers between devices  315 us (49%)
  blocking collectives  83.6 us (13%)
  Pallas kernels  70.2 us (11%)
  matrix products  64.9 us (10%)
  other arithmetic  52.6 us (8%)
  starting transfers between devices  17.4 us (3%)
  between operations  15.1 us (2%)
  local copies, waits for them, and re-layouts  10.3 us (2%)
    psum x1, waiting for transfers between devices, per_device(): mixer_grads = lax.psum((*grads, out_grad), 'seq')  279 us
    pallas_call x4, Pallas kernels, call(): pl.pallas_call(kernel, grid_spec=grid_spec, out_shape=[jax.ShapeDtypeStru...  70.2 us
    psum x1, blocking collectives, per_device(): bias_sum, head_sum = lax.psum((bias_grad[0], head_gain_grad[0]), 'seq')  42.3 us
    psum x1, blocking collectives, per_device(): lax.psum((norm_gain_part, feed_gain_part), ('seq', 'tp'))  41.2 us
    dot_general x8, matrix products, tn(): lax.dot_general(a, b, (((0,), (0,)), ((), ())), preferred_element_type=F32)  27.8 us
    ppermute x8, waiting for transfers between devices, scan_states(): got = lax.ppermute(sent, 'seq', [(i, i ^ 1 << bit) for i in range(count)])  24.6 us
    dot_general x3, matrix products, nt(): lax.dot_general(a, b, (((1,), (1,)), ((), ())), preferred_element_type=F32)  19.5 us
    convert_element_type x8, other arithmetic, per_device(): wide = [g.astype(F32) for g in (*mixer_grads, *ff_grads)]  18.5 us
  transfers between devices with their start and end apart: 17, of which 12 were waited for; matrix products, arithmetic and copies ran while one was open for 7% of the time, Pallas kernels for 0%

profile of v1, /device:TPU:0, one launch (start us, length us, event | category | flops | bytes accessed | tf_op | source)
XLA Modules:
  0.0 628.7 jit_solution(4755260670965238494)
XLA Ops:
  7.8 0.9 fusion.69
  10.4 1.0 broadcast_in_dim.72.code_ref
  11.4 14.3 %project.1 = (bf16[1024,1024]{1,0:T(8,128)(2,1)}, bf16[1024,512]{1,0:T(8,128)(2,1)}, bf16[1024,512]{1,0:T(8,128)(2,1)}, bf16[1024,512]{1,0:T(8,128)(2,1)}, bf16[...) custom-call(s32[1]{0:T(128)} %bitcast.tp_ref, ...), custom_call_target="tpu_custom_call" | custom-call | flops 3489660928 | bytes 16777216 | tf_op jit(solution)/shard_map/project/pallas_call | solution.py:386
  26.7 1.0 convert_element_type.266
  27.7 2.9 collective-permute-start.1
  30.5 0.9 slice_reduce_fusion.11
  31.5 4.3 collective-permute-done.1
  35.7 1.5 subtract_convert_fusion.6
  37.3 1.1 fusion.38
  39.1 1.8 collective-permute-start.2
  41.8 3.9 collective-permute-done.2
  45.8 1.5 multiply_select_fusion.3
  48.3 1.5 collective-permute-start.3
  50.8 3.5 collective-permute-done.3
  55.2 1.5 fusion.26
  56.7 1.2 fusion.18
  58.6 2.5 collective-permute-start.4
  62.1 6.3 %collective-permute-done.4 = bf16[128,768]{1,0:T(8,128)(2,1)} collective-permute-done((bf16[128,768]{1,0:T(8,128)(2,1)}, bf16[128,768]{1,0:T(8,128)(2,1)}, u32[]{:S(2)}, u32[]{:S(2)}) %collective-permute-start.4) | collective-permute-done | bytes 196640 | tf_op jit(solution)/shard_map/ppermute | solution.py:417
  68.4 1.9 add_select_fusion.3.start_ref
  70.3 17.7 %mix.1 = (f32[1024,128]{1,0:T(8,128)}, f32[8,128,512]{2,1,0:T(8,128)}, f32[1024,512]{1,0:T(8,128)}, bf16[1024,512]{1,0:T(8,128)(2,1)}, bf16[512,1024]{1,0:T(8,128)(2,1)}, /*index=5*/bf16[512,1024]{1,0:T(8,128)(2,1)}) custom-call(s32[1]{0:T(128)} %bitcast.tp_ref, bf16[1024,512]{1,0:T(8,128)(2,1)} %get-tuple-element.45.q_ref, ...), custom_call_target="tpu_custom_call" | custom-call | flops 2147483648 | bytes 16777216 | tf_op jit(solution)/shard_map/mix/pallas_call | solution.py:386
  88.6 3.0 collective-permute-done.5
  91.6 1.9 multiply_reduce_fusion.2
  94.2 2.3 collective-permute-done.6
  97.3 6.0 fusion.35
  103.3 6.1 fusion.36
  109.4 10.4 %multiply_convert_fusion = (bf16[1024,1408]{1,0:T(8,128)(2,1)}, bf16[1024,1408]{1,0:T(8,128)(2,1)}, bf16[1024,1408]{1,0:T(8,128)(2,1)}) fusion(f32[1024,1408]{1,0:T(8,128)} %fusion.36, f32[1024,1408]{1,0:T(8,128)} %fusion.35, bf16[1024,1024]{1,0:T(8,128)(2,1)S(1)} %constant_dynamic-update-slice_fusion, bf16[1408,1024]{1,0:T(8,128)(2,1)S(1)} %copy-done), kind=kOutput, calls=%fused_computation | convolution fusion | flops 2975858688 | bytes 25165824 | tf_op jit(solution)/shard_map/dot_general | solution.py:34
  119.8 5.4 fusion.44
  125.3 3.7 add_convert_fusion
  129.2 2.5 collective-permute-done.9
  132.8 1.8 fusion.39.da_own_ref
  134.7 2.9 collective-permute-done.10.da_other_ref
  137.6 15.6 %score.1 = (bf16[1024,1024]{1,0:T(8,128)(2,1)}, bf16[1024,512]{1,0:T(8,128)(2,1)}, f32[1024,128]{1,0:T(8,128)}, f32[1024,128]{1,0:T(8,128)}, f32[1,512]{1,0:T(1,...) custom-call(s32[1]{0:T(128)} %bitcast.tp_ref, bf16[512,1024]{1,0:T(8,128)(2,1)} %fusion.39.da_own_ref, ...), custom_call_target="tpu_custom_call" | custom-call | flops 2147483648 | bytes 16777216 | tf_op jit(solution)/shard_map/score/pallas_call | solution.py:386
  154.1 1.0 convert_element_type.307
  155.1 1.1 collective-permute-start.11
  156.3 6.5 %convolution_convert_fusion = bf16[1408,1024]{1,0:T(8,128)(2,1)} fusion(bf16[1024,1408]{1,0:T(8,128)(2,1)} %get-tuple-element.126, bf16[1024,1024]{1,0:T(8,128)(2,1)S(1)} %copy-done.23), kind=kOutput, calls=%fused_computation.5 | convolution fusion | flops 2954231808 | bytes 7864320 | tf_op jit(solution)/shard_map/dot_general | solution.py:38
  163.3 1.6 collective-permute-start.12
  164.8 4.8 convolution_convert_fusion.1
  171.2 5.0 convolution_convert_fusion.2
  177.1 3.1 collective-permute-start.14
  180.2 2.2 convolution_convert_fusion.4
  182.6 6.0 collective-permute-done.14
  188.5 1.4 multiply_reduce_fusion.3
  189.9 22.6 %grad.1 = (bf16[1024,512]{1,0:T(8,128)(2,1)}, bf16[1024,512]{1,0:T(8,128)(2,1)}, bf16[1024,512]{1,0:T(8,128)(2,1)}, bf16[1024,128]{1,0:T(8,128)(2,1)}, f32[1,128...) custom-call(s32[1]{0:T(128)} %bitcast.tp_ref, bf16[1024,512]{1,0:T(8,128)(2,1)} %get-tuple-element.45.q_ref, ...), custom_call_target="tpu_custom_call" | custom-call | flops 3489660928 | bytes 25165824 | tf_op jit(solution)/shard_map/grad/pallas_call | solution.py:386
  212.5 2.5 convolution_convert_fusion.8
  215.0 2.3 convolution_convert_fusion.7
  217.3 2.2 convolution_convert_fusion.6
  219.5 2.3 convolution_convert_fusion.5
  221.9 5.4 convolution_convert_fusion.3
  227.4 1.3 copy-done.12
  228.7 1.0 slice.189
  230.2 42.3 %all-reduce.1 = (f32[128]{0:T(128)}, f32[512]{0:T(512)}) all-reduce(f32[128]{0:T(128)S(1)} %bitcast.40, f32[512]{0:T(512)S(1)} %bitcast.39), channel_id=1, replica_groups=mesh['seq'=16,'tp'=2] {'seq'}, use_global_device_ids=true, to_apply=%region_15.16 | all-reduce | flops 640 | bytes 5120 | tf_op jit(solution)/shard_map/psum | solution.py:560
  272.5 2.7 fusion.8
  275.2 41.2 %all-reduce = (f32[1024]{0:T(1024)}, f32[1024]{0:T(1024)}) all-reduce(f32[1024]{0:T(1024)S(1)} %get-tuple-element.78, f32[1024]{0:T(1024)S(1)} %get-tuple-element.76), channel_id=1, replica_groups=mesh['seq'=16,'tp'=2] {'seq','tp'}, use_global_device_ids=true, to_apply=%region_10.11 | all-reduce | flops 2048 | bytes 16384 | tf_op jit(solution)/shard_map/psum | solution.py:559
  316.5 5.9 fusion.7
  322.4 279.3 %all-reduce.5.cloned.1.call-done = (bf16[1024,512]{1,0:T(8,128)(2,1)}, bf16[1024,512]{1,0:T(8,128)(2,1)}, bf16[1024,512]{1,0:T(8,128)(2,1)}, bf16[1024,128]{1,0:...) async-done(((bf16[1024,512]{1,0:T(8,128)(2,1)}, bf16[1024,512]{1,0:T(8,128)(2,1)}, ...) | async-done | bytes 13107216 | tf_op jit(solution)/shard_map/psum | solution.py:555
  601.7 1.9 convert_element_type.343
  603.5 2.8 convert_element_type.337
  606.4 1.6 convert_element_type.339
  608.0 1.6 convert_element_type.341
  609.6 1.6 convert_element_type.345
  611.2 1.0 copy-done.11
  612.2 2.9 convert_element_type.347
  615.2 2.9 convert_element_type.349
  618.2 3.2 convert_element_type.351
  (138 shorter events, 17.3 us)
Async XLA Ops:
  7.2 102.2 %copy-start = (bf16[1408,1024]{1,0:T(8,128)(2,1)S(1)}, bf16[1408,1024]{1,0:T(8,128)(2,1)}, u32[]{:S(2)}) copy-start(bf16[1408,1024]{1,0:T(8,128)(2,1)} %param.31) | copy-start | bytes 8650756
  7.2 594.5 %all-reduce.5.cloned.1.call-start = ((), (), s32[]{:S(2)}) async-start(), calls=%async_computation | async-start | bytes 26214400 | tf_op jit(solution)/shard_map/psum | solution.py:555
  7.2 3.2 collective-permute-start
  25.7 21.7 %copy-start.6 = (f32[128,512]{1,0:T(8,128)S(1)}, f32[128,512]{1,0:T(8,128)}, u32[]{:S(2)}) copy-start(f32[128,512]{1,0:T(8,128)} %get-tuple-element.50) | copy-start | bytes 786436
  27.7 8.1 %collective-permute-start.1 = (bf16[128,768]{1,0:T(8,128)(2,1)S(1)}, bf16[128,768]{1,0:T(8,128)(2,1)S(1)}, u32[]{:S(2)}, u32[]{:S(2)}) collective-permute-start(bf16[128,768]{1,0:T(8,128)(2,1)S(1)} %pad_maximum_fusion.1), channel_id=1, source_target_pairs={{0,2},{2,0},{4,6},{6,4},{8,10},{10,8},{12,14},{14,12},{16,18},{18,... | collective-permute-start | bytes 589832 | tf_op jit(solution)/shard_map/ppermute | solution.py:417
  39.1 6.6 %collective-permute-start.2 = (bf16[128,768]{1,0:T(8,128)(2,1)}, bf16[128,768]{1,0:T(8,128)(2,1)S(1)}, u32[]{:S(2)}, u32[]{:S(2)}) collective-permute-start(bf16[128,768]{1,0:T(8,128)(2,1)} %pad_maximum_fusion.2), channel_id=1, source_target_pairs={{0,4},{2,6},{4,0},{6,2},{8,12},{10,14},{12,8},{14,10},{16,20},{18,... | collective-permute-start | bytes 589832 | tf_op jit(solution)/shard_map/ppermute | solution.py:417
  48.3 6.0 collective-permute-start.3
  58.6 9.8 %collective-permute-start.4 = (bf16[128,768]{1,0:T(8,128)(2,1)}, bf16[128,768]{1,0:T(8,128)(2,1)}, u32[]{:S(2)}, u32[]{:S(2)}) collective-permute-start(bf16[128,768]{1,0:T(8,128)(2,1)} %pad_maximum_fusion.4), channel_id=1, source_target_pairs={{0,16},{2,18},{4,20},{6,22},{8,24},{10,26},{12,28},{14,30},{16,0},... | collective-permute-start | bytes 589832 | tf_op jit(solution)/shard_map/ppermute | solution.py:417
  70.3 17.8 %copy-start.4 = (bf16[512,1024]{1,0:T(8,128)(2,1)S(1)}, bf16[512,1024]{1,0:T(8,128)(2,1)}, u32[]{:S(2)}) copy-start(bf16[512,1024]{1,0:T(8,128)(2,1)} %param.33) | copy-start | bytes 3145732
  70.3 21.3 %copy-start.3 = (bf16[512,1024]{1,0:T(8,128)(2,1)S(1)}, bf16[512,1024]{1,0:T(8,128)(2,1)}, u32[]{:S(2)}) copy-start(bf16[512,1024]{1,0:T(8,128)(2,1)} %own_ref.1) | copy-start | bytes 3145732
  88.1 3.6 collective-permute-start.5
  88.2 6.0 collective-permute-start.8
  91.6 1.9 copy-start.24
  93.5 39.1 %copy-start.1 = (f32[512,1024]{1,0:T(8,128)}, f32[512,1024]{1,0:T(8,128)S(1)}, u32[]{:S(2)}) copy-start(f32[512,1024]{1,0:T(8,128)S(1)} %get-tuple-element.113) | copy-start | bytes 6291460
  93.8 9.5 %copy-start.18 = (bf16[512,1024]{1,0:T(8,128)(2,1)}, bf16[512,1024]{1,0:T(8,128)(2,1)S(1)}, u32[]{:S(2)}) copy-start(bf16[512,1024]{1,0:T(8,128)(2,1)S(1)} %multiply_convert_fusion.3) | copy-start | bytes 3145732
  93.8 3.4 copy-start.29
  93.8 2.7 collective-permute-start.6
  94.2 15.2 %copy-start.22 = (bf16[1024,1024]{1,0:T(8,128)(2,1)}, bf16[1024,1024]{1,0:T(8,128)(2,1)S(1)}, u32[]{:S(2)}) copy-start(bf16[1024,1024]{1,0:T(8,128)(2,1)S(1)} %constant_dynamic-update-slice_fusion) | copy-start | bytes 6291460
  94.2 9.1 %copy-start.28 = (bf16[1024,1408]{1,0:T(8,128)(2,1)S(1)}, bf16[1024,1408]{1,0:T(8,128)(2,1)}, u32[]{:S(2)}) copy-start(bf16[1024,1408]{1,0:T(8,128)(2,1)} %param.29) | copy-start | bytes 8650756
  97.3 6.1 copy-start.30
  119.8 5.4 copy-start.36
  129.0 3.7 copy-start.5
  129.1 2.7 collective-permute-start.9
  131.8 1.0 copy-start.2
  134.5 3.0 collective-permute-start.10
  137.6 18.7 %copy-start.23 = (bf16[1024,1024]{1,0:T(8,128)(2,1)S(1)}, bf16[1024,1024]{1,0:T(8,128)(2,1)}, u32[]{:S(2)}) copy-start(bf16[1024,1024]{1,0:T(8,128)(2,1)} %copy-done.22) | copy-start | bytes 6291460
  155.1 7.8 %collective-permute-start.11 = (bf16[128,768]{1,0:T(8,128)(2,1)S(1)}, bf16[128,768]{1,0:T(8,128)(2,1)S(1)}, u32[]{:S(2)}, u32[]{:S(2)}) collective-permute-start(bf16[128,768]{1,0:T(8,128)(2,1)S(1)} %pad_maximum_fusion.5), channel_id=1, source_target_pairs={{0,2},{2,0},{4,6},{6,4},{8,10},{10,8},{12,14},{14,12},{16,18},{18,... | collective-permute-start | bytes 589832 | tf_op jit(solution)/shard_map/ppermute | solution.py:417
  156.3 6.6 %copy-start.21 = (f32[128,128]{1,0:T(8,128)S(1)}, f32[128,128]{1,0:T(8,128)}, u32[]{:S(2)}) copy-start(f32[128,128]{1,0:T(8,128)} %get-tuple-element.64) | copy-start | bytes 196612
  156.3 6.8 %copy-start.8 = (f32[128,512]{1,0:T(8,128)S(1)}, f32[128,512]{1,0:T(8,128)}, u32[]{:S(2)}) copy-start(f32[128,512]{1,0:T(8,128)} %get-tuple-element.63) | copy-start | bytes 786436
  156.3 8.6 %copy-start.19 = (bf16[512,1024]{1,0:T(8,128)(2,1)S(1)}, bf16[512,1024]{1,0:T(8,128)(2,1)}, u32[]{:S(2)}) copy-start(bf16[512,1024]{1,0:T(8,128)(2,1)} %copy-done.18) | copy-start | bytes 3145732
  156.3 8.6 %copy-start.31 = (bf16[512,1024]{1,0:T(8,128)(2,1)S(1)}, bf16[512,1024]{1,0:T(8,128)(2,1)}, u32[]{:S(2)}) copy-start(bf16[512,1024]{1,0:T(8,128)(2,1)} %copy-done.30) | copy-start | bytes 3145732
  156.3 8.6 %copy-start.37 = (bf16[1024,1408]{1,0:T(8,128)(2,1)S(1)}, bf16[1024,1408]{1,0:T(8,128)(2,1)}, u32[]{:S(2)}) copy-start(bf16[1024,1408]{1,0:T(8,128)(2,1)} %get-tuple-element.124) | copy-start | bytes 8650756
  163.3 7.9 %copy-start.35 = (bf16[1024,1408]{1,0:T(8,128)(2,1)S(1)}, bf16[1024,1408]{1,0:T(8,128)(2,1)}, u32[]{:S(2)}) copy-start(bf16[1024,1408]{1,0:T(8,128)(2,1)} %get-tuple-element.125) | copy-start | bytes 8650756
  163.3 6.7 %collective-permute-start.12 = (bf16[128,768]{1,0:T(8,128)(2,1)S(1)}, bf16[128,768]{1,0:T(8,128)(2,1)S(1)}, u32[]{:S(2)}, u32[]{:S(2)}) collective-permute-start(bf16[128,768]{1,0:T(8,128)(2,1)S(1)} %pad_maximum_fusion.6), channel_id=1, source_target_pairs={{0,4},{2,6},{4,0},{6,2},{8,12},{10,14},{12,8},{14,10},{16,20},{18,... | collective-permute-start | bytes 589832 | tf_op jit(solution)/shard_map/ppermute | solution.py:417
  170.4 9.8 %copy-start.13 = (bf16[1024,1024]{1,0:T(8,128)(2,1)S(1)}, bf16[1024,1024]{1,0:T(8,128)(2,1)}, u32[]{:S(2)}) copy-start(bf16[1024,1024]{1,0:T(8,128)(2,1)} %get-tuple-element.75) | copy-start | bytes 6291460
  170.4 9.8 %copy-start.20 = (bf16[1024,512]{1,0:T(8,128)(2,1)S(1)}, bf16[1024,512]{1,0:T(8,128)(2,1)}, u32[]{:S(2)}) copy-start(bf16[1024,512]{1,0:T(8,128)(2,1)} %get-tuple-element.74) | copy-start | bytes 3145732
  170.4 6.2 collective-permute-start.13
  177.1 11.4 %collective-permute-start.14 = (bf16[128,768]{1,0:T(8,128)(2,1)S(1)}, bf16[128,768]{1,0:T(8,128)(2,1)S(1)}, u32[]{:S(2)}, u32[]{:S(2)}) collective-permute-start(bf16[128,768]{1,0:T(8,128)(2,1)S(1)} %pad_maximum_fusion.8), channel_id=1, source_target_pairs={{0,16},{2,18},{4,20},{6,22},{8,24},{10,26},{12,28},{14,30},{16,0},... | collective-permute-start | bytes 589832 | tf_op jit(solution)/shard_map/ppermute | solution.py:417
  180.2 8.3 %copy-start.17 = (f32[128,512]{1,0:T(8,128)S(1)}, f32[128,512]{1,0:T(8,128)}, u32[]{:S(2)}) copy-start(f32[128,512]{1,0:T(8,128)} %add_select_fusion.3.start_ref) | copy-start | bytes 786436
  189.9 22.6 %copy-start.7 = (bf16[1024,1024]{1,0:T(8,128)(2,1)S(1)}, bf16[1024,1024]{1,0:T(8,128)(2,1)}, u32[]{:S(2)}) copy-start(bf16[1024,1024]{1,0:T(8,128)(2,1)} %get-tuple-element.67) | copy-start | bytes 6291460
  212.5 2.5 copy-start.34
  215.0 2.3 copy-start.33
  217.3 2.3 copy-start.32
  221.8 50.7 %collective-permute-start.15 = (bf16[512,1024]{1,0:T(8,128)(2,1)}, bf16[512,1024]{1,0:T(8,128)(2,1)}, u32[]{:S(2)}, u32[]{:S(2)}) collective-permute-start(bf16[512,1024]{1,0:T(8,128)(2,1)} %get-tuple-element.66), channel_id=1, source_target_pairs={{0,1},{1,0},{2,3},{3,2},{4,5},{5,4},{6,7},{7,6},{8,9},{9,8},{10,11... | collective-permute-start | bytes 3145736 | tf_op jit(solution)/shard_map/ppermute | solution.py:407
  227.3 1.3 copy-start.12
  228.7 1.5 copy-start.26
  228.7 1.5 copy-start.27
  228.7 43.9 %copy-start.25 = (f32[1024]{0:T(1024)S(1)}, f32[1024]{0:T(1024)}, u32[]{:S(2)}) copy-start(f32[1024]{0:T(1024)} %param.20) | copy-start | bytes 12292
  229.7 86.8 %collective-permute-start.7 = (bf16[512,1024]{1,0:T(8,128)(2,1)}, bf16[512,1024]{1,0:T(8,128)(2,1)}, u32[]{:S(2)}, u32[]{:S(2)}) collective-permute-start(bf16[512,1024]{1,0:T(8,128)(2,1)} %slice.189), channel_id=1, source_target_pairs={{0,1},{1,0},{2,3},{3,2},{4,5},{5,4},{6,7},{7,6},{8,9},{9,8},{10,11... | collective-permute-start | bytes 3145736 | tf_op jit(solution)/shard_map/ppermute | solution.py:407
  601.7 4.7 copy-start.16
  606.4 1.6 copy-start.15
  608.0 1.6 copy-start.14
  609.6 2.6 copy-start.11
  612.2 3.0 copy-start.10
  615.2 3.0 copy-start.9
Sparse Core Ops, SparseCore 0:
  221.9 379.6 all-reduce.4

commit v2 on v1

--- a/solution.py
+++ b/solution.py
@@ -24,6 +24,8 @@
 BF = jnp.bfloat16
 F32 = jnp.float32
 VMEM_LIMIT = 56 * 1024 * 1024
+UNIT = 1024
+MESH = pl.DeviceIdType.MESH
 
 
 def dot(a, b):
@@ -305,7 +307,7 @@
 def grad_kernel(
     tp_ref, q_ref, k_ref, v_ref, dsq_ref, dsk_ref, gate_ref, weight_ref, dz_ref, logit_ref, kvs_ref, dmix_ref, dl_ref, y_ref,
     end_ref, flow_ref, sums_ref, pairs_ref, flipped_ref, back_ref, wq_ref, wk_ref, wv_ref, wf_ref,
-    dq_ref, dk_ref, dv_ref, df_ref, bias_ref, own_ref, other_ref, dkv_ref, carry_ref,
+    d_ref, bias_ref, own_ref, other_ref, dkv_ref, carry_ref,
 ):
     step = pl.program_id(0)
 
@@ -349,7 +351,7 @@
     late = lax.broadcasted_iota(jnp.int32, gate.shape, 0) >= BUCKET
     flow = jnp.where(cut, both[CH:], both[:CH]) + jnp.where(cut & jnp.logical_not(late), 0.0, carry_ref[...])
     df = ((flow - jnp.exp(gate) * dw) * dz_ref[...]).astype(BF)
-    dq_ref[...], dk_ref[...], dv_ref[...], df_ref[...] = dq, dk, dv, df
+    d_ref[...] = jnp.concatenate([dq, dk, dv, df], 1)
     bias_part = jnp.sum(df.astype(F32), axis=0, keepdims=True)
     new = fade_of(gate) * dkv + state_grads(dl, probs, first, q, dmix)
     dkv_ref[...] = new
@@ -373,6 +375,238 @@
     @pl.when(step > 0)
     def _():
         bias_ref[...] += bias_part
+
+
+def line_sizes(count):
+    return {16: (2, 2, 4), 64: (4, 4, 4)}.get(count, (count, 1, 1))
+
+
+def reduce_kernel(sizes, jobs, slots_of, *refs):
+    arrays = len({a for a, *_ in jobs})
+    small_ref, ins, small_out, outs = refs[0], refs[1 : arrays + 1], refs[arrays + 1], refs[arrays + 2 : 2 * arrays + 2]
+    rest = list(refs[2 * arrays + 2 :])
+    small_held, small_got, small_send, small_recv, send_sem, recv_sem, local_sem = rest[-7:]
+    index = lax.axis_index("seq")
+    strides = (1, sizes[0], sizes[0] * sizes[1])
+    place = [lax.rem(index // s, m) for s, m in zip(strides, sizes)]
+
+    def peer(axis, d):
+        m = sizes[axis]
+        return index + (lax.rem(place[axis] + d, m) - place[axis]) * strides[axis]
+
+    barrier = pltpu.get_barrier_semaphore()
+    partners = [(axis, d) for axis in range(3) for d in range(1, sizes[axis])]
+    for axis, d in partners:
+        pl.semaphore_signal(barrier, inc=1, device_id={"seq": peer(axis, d)}, device_id_type=MESH)
+    pl.semaphore_wait(barrier, len(partners))
+
+    work = []
+    for a, first, units, order in jobs:
+        shape = []
+        rows, offset = UNIT, 0
+        for axis in order:
+            rows = rows // sizes[axis]
+            offset = offset + place[axis] * rows
+            shape.append((axis, rows, pl.multiple_of(place[axis] * rows, 16), pl.multiple_of(offset, 16)))
+        held, got = [], []
+        for _ in range(3):
+            held.append(rest.pop(0))
+            got.append(rest.pop(0))
+        own = rest.pop(0)
+        work.append((ins[a], outs[a], pl.ds(first, units), units, shape, held, got, own))
+
+    pending = []
+
+    def remote(j, stage, axis, d, src, dst):
+        return pltpu.make_async_remote_copy(
+            src_ref=src, dst_ref=dst, send_sem=send_sem.at[j, stage, d - 1], recv_sem=recv_sem.at[j, stage, d - 1],
+            device_id={"seq": peer(axis, d)}, device_id_type=MESH,
+        )
+
+    flight = {}
+
+    def scatter(j, stage):
+        src, _, at, units, shape, held, got, own = work[j]
+        axis, rows, _, _ = shape[stage]
+        if stage == 0:
+            copy = pltpu.make_async_copy(
+                src.at[at, pl.ds(shape[0][2], rows), :], own, local_sem.at[j, 0]
+            )
+            copy.start()
+            flight[j, "own"] = copy
+        else:
+            src, at = held[stage - 1], slice(None)
+        flight[j, stage] = []
+        for d in range(1, sizes[axis]):
+            target = pl.multiple_of(lax.rem(place[axis] + d, sizes[axis]) * rows, 16)
+            copy = remote(j, stage, axis, d, src.at[at, pl.ds(target, rows), :], got[stage].at[d - 1])
+            copy.start()
+            flight[j, stage].append(copy)
+
+    def add(j, stage):
+        _, out, at, units, shape, held, got, own = work[j]
+        axis, rows, mine, _ = shape[stage]
+        if stage == 0:
+            flight[j, "own"].wait()
+        for copy in flight[j, stage]:
+            copy.wait_recv()
+
+        def one(u, _):
+            if stage == 0:
+                total = own[u].astype(F32)
+            else:
+                total = held[stage - 1][u, pl.ds(mine, rows), :].astype(F32)
+            for d in range(sizes[axis] - 1):
+                total = total + got[stage][d, u].astype(F32)
+            held[stage][u] = total.astype(BF)
+            return 0
+
+        lax.fori_loop(0, units, one, 0)
+
+    def gather(j, stage):
+        _, out, at, units, shape, held, got, own = work[j]
+        axis, rows, _, offset = shape[stage]
+        here = out.at[at, pl.ds(offset, rows), :]
+        src = here
+        if stage == 2:
+            src = held[2]
+            copy = pltpu.make_async_copy(src, here, local_sem.at[j, 1])
+            copy.start()
+            flight[j, "home"] = copy
+        flight[j, 5 - stage] = []
+        for d in range(1, sizes[axis]):
+            copy = remote(j, 5 - stage, axis, d, src, here)
+            copy.start()
+            flight[j, 5 - stage].append(copy)
+
+    def landed(j, stage):
+        if stage == 2:
+            flight[j, "home"].wait()
+        for copy in flight[j, 5 - stage]:
+            copy.wait_recv()
+
+    def step(j, s):
+        if s == 0:
+            scatter(j, 0)
+        elif s <= 2:
+            add(j, s - 1)
+            scatter(j, s)
+        elif s == 3:
+            add(j, 2)
+            gather(j, 2)
+        elif s <= 5:
+            landed(j, 6 - s)
+            gather(j, 5 - s)
+        else:
+            landed(j, 0)
+
+    def small_step(s):
+        if s > 0:
+            total = small_held[s - 1]
+            for copy in flight["small", s - 1]:
+                copy.wait_recv()
+            for d in range(sizes[s - 1] - 1):
+                total = total + small_got[s - 1, d]
+            if s == 3:
+                small_out[...] = total
+                return
+            small_held[s] = total
+        else:
+            small_held[0] = small_ref[...]
+        flight["small", s] = []
+        for d in range(1, sizes[s]):
+            copy = pltpu.make_async_remote_copy(
+                src_ref=small_held.at[s], dst_ref=small_got.at[s, d - 1], send_sem=small_send.at[s, d - 1],
+                recv_sem=small_recv.at[s, d - 1], device_id={"seq": peer(s, d)}, device_id_type=MESH,
+            )
+            copy.start()
+            flight["small", s].append(copy)
+
+    for slot in range(max(slots_of) + 7):
+        if slot <= 3:
+            small_step(slot)
+        for j, begin in enumerate(slots_of):
+            if 0 <= slot - begin <= 6:
+                step(j, slot - begin)
+    for copies in flight.values():
+        if isinstance(copies, list):
+            for copy in copies:
+                copy.wait_send()
+
+
+def reduce_units(small, arrays, jobs, slots_of):
+    sizes = line_sizes(lax.axis_size("seq"))
+    scratch = []
+    for _, _, units, order in jobs:
+        rows = UNIT
+        for axis in order:
+            rows = rows // sizes[axis]
+            scratch.append(pltpu.VMEM((units, rows, 128), BF))
+            scratch.append(pltpu.VMEM((max(sizes[axis] - 1, 1), units, rows, 128), BF))
+        scratch.append(pltpu.VMEM((units, UNIT // sizes[order[0]], 128), BF))
+    most = max(max(sizes) - 1, 1)
+    scratch += [pltpu.VMEM((3, *small.shape), F32), pltpu.VMEM((3, most, *small.shape), F32)]
+    scratch += [pltpu.SemaphoreType.DMA((3, most))] * 2
+    scratch += [pltpu.SemaphoreType.DMA((len(jobs), 6, most))] * 2 + [pltpu.SemaphoreType.DMA((len(jobs), 2))]
+    return pl.pallas_call(
+        functools.partial(reduce_kernel, sizes, jobs, slots_of),
+        out_shape=[jax.ShapeDtypeStruct(small.shape, F32)] + [jax.ShapeDtypeStruct(a.shape, BF) for a in arrays],
+        in_specs=[pl.BlockSpec(memory_space=pltpu.VMEM)] + [pl.BlockSpec(memory_space=pl.ANY)] * len(arrays),
+        out_specs=[pl.BlockSpec(memory_space=pltpu.VMEM)] + [pl.BlockSpec(memory_space=pl.ANY)] * len(arrays),
+        scratch_shapes=scratch,
+        compiler_params=pltpu.CompilerParams(
+            collective_id=0, has_side_effects=True, vmem_limit_bytes=VMEM_LIMIT
+        ),
+        name="reduce",
+    )(small, *arrays)
+
+
+def units_kernel(a_ref, b_ref, out_ref):
+    part = tn(a_ref[...], b_ref[...]).astype(BF)
+    for c in range(out_ref.shape[0]):
+        out_ref[c] = part[:, c * 128 : (c + 1) * 128]
+
+
+def outer_units(a, b, name):
+    span, tall = a.shape
+    steps = -(-b.shape[1] // 512)
+    return pl.pallas_call(
+        units_kernel,
+        grid=(steps,),
+        in_specs=[pl.BlockSpec((span, tall), lambda i: (0, 0)), pl.BlockSpec((span, 512), lambda i: (0, i))],
+        out_specs=pl.BlockSpec((4, tall, 128), lambda i: (i, 0, 0)),
+        out_shape=jax.ShapeDtypeStruct((4 * steps, tall, 128), BF),
+        compiler_params=pltpu.CompilerParams(dimension_semantics=("arbitrary",), vmem_limit_bytes=VMEM_LIMIT),
+        cost_estimate=pl.CostEstimate(flops=2 * span * tall * b.shape[1], bytes_accessed=8 << 20, transcendentals=0),
+        name=name,
+    )(a, b)
+
+
+def widen_kernel(parts, *refs):
+    for (which, first, count), out_ref in zip(parts, refs[-len(parts) :]):
+        for c in range(count):
+            out_ref[:, c * 128 : (c + 1) * 128] = refs[which][first + c].astype(F32)
+
+
+def widen(arrays, parts, steps, name):
+    spec = lambda shape, index: pl.BlockSpec(shape, index)
+    return pl.pallas_call(
+        functools.partial(widen_kernel, parts),
+        grid=(steps,),
+        in_specs=[spec((a.shape[0], a.shape[1] // steps, 128), lambda i: (0, i, 0)) for a in arrays],
+        out_specs=[spec((arrays[w].shape[1] // steps, n * 128), lambda i: (i, 0)) for w, _, n in parts],
+        out_shape=[jax.ShapeDtypeStruct((arrays[w].shape[1], n * 128), F32) for w, _, n in parts],
+        compiler_params=pltpu.CompilerParams(dimension_semantics=("arbitrary",), vmem_limit_bytes=VMEM_LIMIT),
+        name=name,
+    )(*arrays)
+
+
+X, Y, Z = 0, 1, 2
+PLAN = (
+    (1, 0, 2, (Y, X, Z), 2), (2, 0, 6, (X, Y, Z), 1), (0, 0, 8, (X, Y, Z), 2), (0, 8, 6, (Y, X, Z), 2),
+    (1, 2, 9, (X, Y, Z), 3), (0, 14, 8, (Y, X, Z), 3), (2, 6, 3, (Z, X, Y), 2), (2, 9, 1, (Y, X, Z), 3),
+    (2, 10, 1, (Y, X, Z), 0), (2, 11, 2, (Z, Y, X), 1), (3, 0, 4, (Y, X, Z), 0),
+)
 
 
 def call(kernel, count, ins, outs, scratch=(), tp=None, flops=0, moved=0, name=None):
@@ -508,10 +742,8 @@
     dup = (dact * ff_gate * sig).astype(BF)
     feed = dot(act, down_weight).astype(BF)
     dhidden = (nt(dgate, gate_weight) + nt(dup, up_weight)).astype(BF)
-    down_grad = tn(act, cot).astype(BF)
-    gate_grad = tn(hidden, dgate).astype(BF)
-    up_grad = tn(hidden, dup).astype(BF)
-    ff_grads = lax.psum((gate_grad, up_grad, down_grad), "seq")
+    down_units = outer_units(act, cot, "down_units")
+    ff_units = outer_units(hidden, jnp.concatenate([dgate, dup], 1), "ff_units")
 
     dhidden_own = dhidden[:half].astype(F32) + swap(dhidden[half:]).astype(F32)
     block_out = (resid + (feed[:half].astype(F32) + swap(feed[half:]).astype(F32))).astype(BF)
@@ -531,37 +763,52 @@
     )
 
     dkv_end = scan_states(dkv_run, reach, False)
-    out_grad = tn(normed, da).astype(BF)
+    out_units = outer_units(normed, da, "out_units")
     kv_end = fade_run[:, :1] * kv_start + kv_run
     flow = jnp.sum(kv_end * dkv_end, axis=1)[None]
 
     turn = lambda i: count - 1 - i
     rows_back = lambda a: (a, (CH, a.shape[1]), lambda i, tp: (turn(i), 0))
     row_back = lambda n, d: ((span, n), d, (CH, n), lambda i, tp: (turn(i), 0))
-    dq, dk, dv, df, bias_grad, dx_own, dx_other = call(
+    d_all, bias_grad, dx_own, dx_other = call(
         grad_kernel, count,
         [rows_back(a) for a in (q, k, v, dsq, dsk, gate, weight, dzf, logits)]
         + [(kvs, (1, lanes, 2 * DH), lambda i, tp: (turn(i), 0, 0)), rows_back(dmix), rows_back(dl), rows_back(y),
            whole(dkv_end), whole(flow), whole(sums), whole(pairs), whole(flipped), whole(back),
            whole(query_weight), whole(key_weight), whole(value_weight), whole(forget_weight)],
-        [row_back(cols, BF)] * 3 + [row_back(lanes, BF), fixed((1, lanes)),
+        [row_back(3 * cols + lanes, BF), fixed((1, lanes)),
          ((half, width), BF, block, lambda i, tp: own_map(turn(i), tp)),
          ((half, width), BF, block, lambda i, tp: other_map(turn(i), tp))],
         scratch=[pltpu.VMEM((lanes, 2 * DH), F32), pltpu.VMEM((1, lanes), F32)],
         tp=tp, flops=2 * span * width * (3 * cols + lanes), moved=24 << 20, name="grad",
     )
 
-    grads = [tn(xn, d).astype(BF) for d in (dq, dk, dv, df)]
-    mixer_grads = lax.psum((*grads, out_grad), "seq")
+    mixer_units = outer_units(xn, d_all, "mixer_units")
     dx = dx_own.astype(F32) + swap(dx_other).astype(F32)
     own_grad, norm_gain_part = row_norm_back(own, norm_gain, dx)
     tokens_grad = (dresid + own_grad).astype(BF)
-    norm_gain_grad, feed_gain_grad = lax.psum((norm_gain_part, feed_gain_part), ("seq", "tp"))
-    bias_sum, head_sum = lax.psum((bias_grad[0], head_gain_grad[0]), "seq")
-    wide = [g.astype(F32) for g in (*mixer_grads, *ff_grads)]
+    small = jnp.concatenate([norm_gain_part, feed_gain_part, bias_grad[0], head_gain_grad[0]]).reshape(-1, 128)
+    small = jnp.pad(small, ((0, -small.shape[0] % 8), (0, 0)))
+
+    def stacked(units):
+        return units.reshape(-1, UNIT, 128)
+
+    small_sum, ff_sum, down_sum, mixer_sum, out_sum = reduce_units(
+        small, [ff_units, stacked(down_units), mixer_units, stacked(out_units)],
+        tuple(p[:4] for p in PLAN), tuple(p[4] for p in PLAN),
+    )
+    vectors = small_sum.reshape(-1)[: 2 * width + lanes + cols]
+    gains = vectors[: 2 * width].reshape(2, width)
+    gains = gains + swap(gains)
+    blocks, ff_blocks = cols // 128, gate_weight.shape[1] // 128
+    gate_sum, up_sum = widen([ff_sum], ((0, 0, ff_blocks), (0, ff_blocks, ff_blocks)), 8, "wide_ff")
+    (down_sum,) = widen([down_sum.reshape(down_units.shape)], ((0, 0, width // 128),), 4, "wide_down")
+    parts = tuple((0, i * blocks, blocks) for i in range(3)) + ((0, 3 * blocks, 1),)
+    query_sum, key_sum, value_sum, forget_sum = widen([mixer_sum], parts, 4, "wide_mixer")
+    (out_sum,) = widen([out_sum.reshape(out_units.shape)], ((0, 0, width // 128),), 2, "wide_out")
     return (
-        block_out, tokens_grad, norm_gain_grad, wide[0], wide[1], wide[2], wide[3], bias_sum, head_sum, wide[4],
-        feed_gain_grad, wide[5], wide[6], wide[7],
+        block_out, tokens_grad, gains[0], query_sum, key_sum, value_sum, forget_sum,
+        vectors[2 * width : 2 * width + lanes], vectors[2 * width + lanes :], out_sum, gains[1], gate_sum, up_sum, down_sum,
     )
 
 

time: 639 us -> 484 us (0.76)
  waiting for transfers between devices: 315 us -> 35.9 us
  Pallas kernels: 70.2 us -> 340 us
  blocking collectives: 83.6 us -> 0 us
  matrix products: 64.9 us -> 34.2 us
  other arithmetic: 52.6 us -> 37.4 us
  between operations: 15.1 us -> 1.21 us
    psum x1 -> x0, waiting for transfers between devices: 279 us -> none  [per_device(): mixer_grads = lax.psum((*grads, out_grad), 'seq')]
    pallas_call x0 -> x9, Pallas kernels: none -> 269 us  [the longest x1 217 us: reduce_units(): pl.pallas_call(functools.partial(reduce_kernel, sizes, jobs, slots_of), o...]
    psum x2 -> x0, blocking collectives: 83.6 us -> none  [the longest x1 42.3 us: per_device(): bias_sum, head_sum = lax.psum((bias_grad[0], head_gain_grad[0]), 'seq')]
    dot_general x8 -> x0, matrix products: 27.8 us -> none  [tn(): lax.dot_general(a, b, (((0,), (0,)), ((), ())), preferred_element_type=F32)]
    convert_element_type x8 -> x0, other arithmetic: 18.5 us -> none  [per_device(): wide = [g.astype(F32) for g in (*mixer_grads, *ff_grads)]]
  transfers between devices with their start and end apart: 17 -> 17, of which waited for: 12 -> 10; matrix products, arithmetic and copies ran while one was open for 7% -> 7% of each run, Pallas kernels for 0% -> 61%
where the time goes in v2:
time: 484 us; the launch traced here: 477 us
  Pallas kernels  340 us (70%)
  other arithmetic  37.4 us (8%)
  waiting for transfers between devices  35.9 us (7%)
  matrix products  34.2 us (7%)
  starting transfers between devices  16.2 us (3%)
  local copies, waits for them, and re-layouts  13 us (3%)
    pallas_call x1, Pallas kernels, reduce_units(): pl.pallas_call(functools.partial(reduce_kernel, sizes, jobs, slots_of), o...  217 us
    pallas_call x4, Pallas kernels, call(): pl.pallas_call(kernel, grid_spec=grid_spec, out_shape=[jax.ShapeDtypeStru...  70.4 us
    pallas_call x4, Pallas kernels, outer_units(): pl.pallas_call(units_kernel, grid=(steps,), in_specs=[pl.BlockSpec((span,...  30.3 us
    ppermute x8, waiting for transfers between devices, scan_states(): got = lax.ppermute(sent, 'seq', [(i, i ^ 1 << bit) for i in range(count)])  25.2 us
    pallas_call x4, Pallas kernels, widen(): pl.pallas_call(functools.partial(widen_kernel, parts), grid=(steps,), in_...  21.7 us
    dot_general x3, matrix products, dot(): lax.dot_general(a, b, (((1,), (0,)), ((), ())), preferred_element_type=F32)  17.7 us
    dot_general x3, matrix products, nt(): lax.dot_general(a, b, (((1,), (1,)), ((), ())), preferred_element_type=F32)  16.5 us
    ppermute x8, starting transfers between devices, scan_states(): got = lax.ppermute(sent, 'seq', [(i, i ^ 1 << bit) for i in range(count)])  14 us
  transfers between devices with their start and end apart: 17, of which 10 were waited for; matrix products, arithmetic and copies ran while one was open for 7% of the time, Pallas kernels for 61%

profile of v2, /device:TPU:0, one launch (start us, length us, event | category | flops | bytes accessed | tf_op | source)
XLA Modules:
  0.0 477.5 jit_solution(954145100810545430)
XLA Ops:
  1.2 0.9 fusion.56
  3.8 1.0 broadcast_in_dim.72.code_ref
  4.8 14.3 %project.1 = (bf16[1024,1024]{1,0:T(8,128)(2,1)}, bf16[1024,512]{1,0:T(8,128)(2,1)}, bf16[1024,512]{1,0:T(8,128)(2,1)}, bf16[1024,512]{1,0:T(8,128)(2,1)}, bf16[...) custom-call(s32[1]{0:T(128)} %bitcast.tp_ref, ...), custom_call_target="tpu_custom_call" | custom-call | flops 3489660928 | bytes 16777216 | tf_op jit(solution)/shard_map/project/pallas_call | solution.py:620
  19.1 0.9 subtract_convert_fusion.7
  20.1 1.0 convert_element_type.220
  21.1 2.9 collective-permute-start.1
  24.0 0.9 slice_reduce_fusion.11
  24.9 4.3 collective-permute-done.1
  29.2 1.5 subtract_convert_fusion.6
  30.8 1.1 fusion.36
  32.5 1.8 collective-permute-start.2
  34.3 0.9 slice_reduce_fusion.8
  35.3 3.9 collective-permute-done.2
  39.2 1.5 multiply_select_fusion.3
  41.7 1.5 collective-permute-start.3
  43.2 0.9 slice_reduce_fusion.6
  44.2 3.6 collective-permute-done.3
  47.7 0.9 multiply_convert_fusion.5
  48.6 1.5 fusion.26
  50.1 1.2 fusion.18
  52.0 2.5 collective-permute-start.4
  54.5 0.9 slice_reduce_fusion.5
  55.5 6.4 %collective-permute-done.4 = bf16[128,768]{1,0:T(8,128)(2,1)} collective-permute-done((bf16[128,768]{1,0:T(8,128)(2,1)}, bf16[128,768]{1,0:T(8,128)(2,1)}, u32[]{:S(2)}, u32[]{:S(2)}) %collective-permute-start.4) | collective-permute-done | bytes 196640 | tf_op jit(solution)/shard_map/ppermute | solution.py:651
  61.8 1.9 add_select_fusion.3.start_ref
  63.8 17.7 %mix.1 = (f32[1024,128]{1,0:T(8,128)}, f32[8,128,512]{2,1,0:T(8,128)}, f32[1024,512]{1,0:T(8,128)}, bf16[1024,512]{1,0:T(8,128)(2,1)}, bf16[512,1024]{1,0:T(8,128)(2,1)}, /*index=5*/bf16[512,1024]{1,0:T(8,128)(2,1)}) custom-call(s32[1]{0:T(128)} %bitcast.tp_ref, bf16[1024,512]{1,0:T(8,128)(2,1)} %get-tuple-element.53.q_ref, ...), custom_call_target="tpu_custom_call" | custom-call | flops 2147483648 | bytes 16777216 | tf_op jit(solution)/shard_map/mix/pallas_call | solution.py:620
  82.1 3.0 collective-permute-done.5
  85.1 1.9 multiply_reduce_fusion.2
  87.7 2.3 collective-permute-done.6
  90.7 6.1 %fusion.39 = f32[1024,1408]{1,0:T(8,128)} fusion(bf16[1024,1408]{1,0:T(8,128)(2,1)S(1)} %copy-done.29, bf16[512,1024]{1,0:T(8,128)(2,1)S(1)} %collective-permute-done.6, bf16[512,1024]{1,0:T(8,128)(2,1)S(1)} %multiply_convert_fusion.3), kind=kOutput, calls=%fused_computation.150 | convolution fusion | flops 2956984320 | bytes 10747904 | tf_op jit(solution)/shard_map/dot_general | solution.py:32
  96.8 6.1 %fusion.38 = f32[1024,1408]{1,0:T(8,128)} fusion(bf16[1024,1408]{1,0:T(8,128)(2,1)S(1)} %copy-done.30, bf16[512,1024]{1,0:T(8,128)(2,1)S(1)} %collective-permute-done.6, bf16[512,1024]{1,0:T(8,128)(2,1)S(1)} %multiply_convert_fusion.3), kind=kOutput, calls=%fused_computation.149 | convolution fusion | flops 2956984320 | bytes 10747904 | tf_op jit(solution)/shard_map/dot_general | solution.py:32
  102.9 9.3 %multiply_convert_fusion = (bf16[1024,1408]{1,0:T(8,128)(2,1)S(1)}, bf16[1024,1408]{1,0:T(8,128)(2,1)S(1)}, bf16[1024,1408]{1,0:T(8,128)(2,1)}) fusion(f32[1024,1408]{1,0:T(8,128)} %fusion.39, f32[1024,1408]{1,0:T(8,128)} %fusion.38, bf16[1024,1024]{1,0:T(8,128)(2,1)S(1)} %constant_dynamic-update-slice_fusion.b_ref, bf16[1408,1024]{1,0:T(8,128)(2,1)S(1)} %copy-done), kind=kOutput, calls=%fused_computation.1 | convolution fusion | flops 2975858688 | bytes 25165824 | tf_op jit(solution)/shard_map/dot_general | solution.py:36
  112.2 3.4 fusion.45
  115.7 3.7 add_convert_fusion
  119.6 2.5 collective-permute-done.9
  123.2 1.8 fusion.37.da_own_ref
  125.1 2.9 collective-permute-done.10.da_other_ref
  128.0 15.5 %score.1 = (bf16[1024,1024]{1,0:T(8,128)(2,1)}, bf16[1024,512]{1,0:T(8,128)(2,1)}, f32[1024,128]{1,0:T(8,128)}, f32[1024,128]{1,0:T(8,128)}, f32[1,512]{1,0:T(1,...) custom-call(s32[1]{0:T(128)} %bitcast.tp_ref, bf16[512,1024]{1,0:T(8,128)(2,1)} %fusion.37.da_own_ref, ...), custom_call_target="tpu_custom_call" | custom-call | flops 2147483648 | bytes 16777216 | tf_op jit(solution)/shard_map/score/pallas_call | solution.py:620
  143.5 0.9 subtract_convert_fusion.3
  144.4 1.0 convert_element_type.261
  145.4 1.1 collective-permute-start.11
  146.6 0.9 slice_reduce_fusion.10
  147.5 4.9 %collective-permute-done.11 = bf16[128,768]{1,0:T(8,128)(2,1)S(1)} collective-permute-done((bf16[128,768]{1,0:T(8,128)(2,1)S(1)}, bf16[128,768]{1,0:T(8,128)(2,1)S(1)}, u32[]{:S(2)}, u32[]{:S(2)}) %collective-permute-start.11) | collective-permute-done | bytes 196640 | tf_op jit(solution)/shard_map/ppermute | solution.py:651
  153.4 1.1 fusion.35
  154.5 1.2 collective-permute-start.12
  155.7 5.6 %convolution_convert_fusion = bf16[1024,1024]{1,0:T(8,128)(2,1)S(1)} fusion(bf16[1024,1408]{1,0:T(8,128)(2,1)} %get-tuple-element.130.a_ref, bf16[1408,1024]{1,0:T(8,128)(2,1)S(1)} %copy-done), kind=kOutput, calls=%fused_computation.30 | convolution fusion | flops 2953838592 | bytes 7864320 | tf_op jit(solution)/shard_map/dot_general | solution.py:32
  162.5 2.9 pad_maximum_fusion.b_ref
  165.5 2.2 collective-permute-done.13
  168.2 2.4 collective-permute-start.14
  170.5 6.7 %down_units.1 = bf16[8,1408,128]{2,1,0:T(8,128)(2,1)} custom-call(bf16[1024,1408]{1,0:T(8,128)(2,1)} %get-tuple-element.130.a_ref, bf16[1024,1024]{1,0:T(8,128)(2,1)} %copy-done.24), custom_call_target="tpu_custom_call" | custom-call | flops 2952790016 | bytes 8388608 | tf_op jit(solution)/shard_map/down_units/pallas_call | solution.py:573
  177.2 1.1 slice.223
  178.4 1.4 multiply_reduce_fusion.3
  179.8 22.9 %grad.1 = (bf16[1024,1664]{1,0:T(8,128)(2,1)}, f32[1,128]{1,0:T(1,128)}, bf16[512,1024]{1,0:T(8,128)(2,1)}, bf16[512,1024]{1,0:T(8,128)(2,1)}) custom-call(s32[1]{0:T(128)} %bitcast.tp_ref, bf16[1024,512]{1,0:T(8,128)(2,1)} %get-tuple-element.53.q_ref, bf16[1024,512]{1,0:T(8,128)(2,1)} %get-tuple-element.54.k_ref, ...), custom_call_target="tpu_custom_call" | custom-call | flops 3489660928 | bytes 25165824 | tf_op jit(solution)/shard_map/grad/pallas_call | solution.py:620
  203.3 1.5 pad_maximum_fusion.1.a_ref
  204.8 11.3 %ff_units.1.refs_1_ = bf16[24,1024,128]{2,1,0:T(8,128)(2,1)} custom-call(bf16[1024,1024]{1,0:T(8,128)(2,1)} %pad_maximum_fusion.1.a_ref, bf16[1024,2816]{1,0:T(8,128)(2,1)} %pad_maximum_fusion.b_ref), custom_call_target="tpu_custom_call" | custom-call | flops 5905580032 | bytes 8388608 | tf_op jit(solution)/shard_map/ff_units/pallas_call | solution.py:573
  216.1 3.8 out_units.1
  219.9 8.5 %mixer_units.1.refs_3_ = bf16[16,1024,128]{2,1,0:T(8,128)(2,1)} custom-call(bf16[1024,1024]{1,0:T(8,128)(2,1)} %get-tuple-element.77.a_ref, bf16[1024,1664]{1,0:T(8,128)(2,1)} %get-tuple-element.78.b_ref), custom_call_target="tpu_custom_call" | custom-call | flops 3489660928 | bytes 8388608 | tf_op jit(solution)/shard_map/mixer_units/pallas_call | solution.py:573
  230.0 217.0 %reduce.37 = (f32[24,128]{1,0:T(8,128)}, bf16[24,1024,128]{2,1,0:T(8,128)(2,1)}, bf16[11,1024,128]{2,1,0:T(8,128)(2,1)}, bf16[16,1024,128]{2,1,0:T(8,128)(2,1)}, bf16[4,1024,128]{2,1,0:T(8,128)(2,1)}) custom-call(f32[24,128]{1,0:T(8,128)} %pad.4.refs_0_, bf16[24,1024,128]{2,1,0:T(8,128)(2,1)} %ff_units.1.refs_1_, bf16[11,1024,128]{2,1,0:T(8,128)(2,1)} %bitcast.35, ...), custom_call_target="tpu_custom_call" | custom-call | tf_op jit(solution)/shard_map/reduce/pallas_call | solution.py:551
  447.8 1.3 slice_bitcast_fusion
  449.0 4.9 %fusion.7 = (bf16[512,1024]{1,0:T(8,128)(2,1)}, bf16[512,1024]{1,0:T(8,128)(2,1)}) fusion(bf16[512,1024]{1,0:T(8,128)(2,1)} %own_ref.1, bf16[512,1024]{1,0:T(8,128)(2,1)} %copy-done.12, bf16[512,1024]{1,0:T(8,128)(2,1)} %get-tuple-element.73, f32[512]{0:T(512)S(1)} %broadcast_multiply_fusion, f32[1024]{0:T(1024)S(1)} %copy-done.26, ...), kind=kLoop, calls=%fused_computation.16 | loop fusion | flops 13631488 | bytes 12599296 | tf_op jit(solution)/shard_map/convert_element_type | solution.py:789
  454.0 1.2 slice_bitcast_fusion.1
  455.1 2.5 wide_out.1
  457.6 5.5 %wide_mixer.1 = (f32[1024,512]{1,0:T(8,128)}, f32[1024,512]{1,0:T(8,128)}, f32[1024,512]{1,0:T(8,128)}, f32[1024,128]{1,0:T(8,128)}) custom-call(bf16[16,1024,128]{2,1,0:T(8,128)(2,1)} %get-tuple-element.82.refs_0_), custom_call_target="tpu_custom_call" | custom-call | tf_op jit(solution)/shard_map/wide_mixer/pallas_call | solution.py:593
  463.1 5.0 %wide_down.1 = f32[1408,1024]{1,0:T(8,128)} custom-call(bf16[8,1408,128]{2,1,0:T(8,128)(2,1)} %bitcast.34), custom_call_target="tpu_custom_call" | custom-call | tf_op jit(solution)/shard_map/wide_down/pallas_call | solution.py:593
  468.1 8.8 %wide_ff.1 = (f32[1024,1408]{1,0:T(8,128)}, f32[1024,1408]{1,0:T(8,128)}) custom-call(bf16[24,1024,128]{2,1,0:T(8,128)(2,1)} %get-tuple-element.88.refs_0_), custom_call_target="tpu_custom_call" | custom-call | tf_op jit(solution)/shard_map/wide_ff/pallas_call | solution.py:593
  (124 shorter events, 14.2 us)
Async XLA Ops:
  0.6 102.2 %copy-start = (bf16[1408,1024]{1,0:T(8,128)(2,1)S(1)}, bf16[1408,1024]{1,0:T(8,128)(2,1)}, u32[]{:S(2)}) copy-start(bf16[1408,1024]{1,0:T(8,128)(2,1)} %param.31) | copy-start | bytes 8650756
  0.7 3.2 collective-permute-start
  19.1 21.7 %copy-start.10 = (f32[128,512]{1,0:T(8,128)S(1)}, f32[128,512]{1,0:T(8,128)}, u32[]{:S(2)}) copy-start(f32[128,512]{1,0:T(8,128)} %get-tuple-element.58) | copy-start | bytes 786436
  21.1 8.1 %collective-permute-start.1 = (bf16[128,768]{1,0:T(8,128)(2,1)S(1)}, bf16[128,768]{1,0:T(8,128)(2,1)S(1)}, u32[]{:S(2)}, u32[]{:S(2)}) collective-permute-start(bf16[128,768]{1,0:T(8,128)(2,1)S(1)} %pad_maximum_fusion.2), channel_id=1, source_target_pairs={{0,2},{2,0},{4,6},{6,4},{8,10},{10,8},{12,14},{14,12},{16,18},{18,... | collective-permute-start | bytes 589832 | tf_op jit(solution)/shard_map/ppermute | solution.py:651
  32.5 6.6 %collective-permute-start.2 = (bf16[128,768]{1,0:T(8,128)(2,1)}, bf16[128,768]{1,0:T(8,128)(2,1)S(1)}, u32[]{:S(2)}, u32[]{:S(2)}) collective-permute-start(bf16[128,768]{1,0:T(8,128)(2,1)} %pad_maximum_fusion.3), channel_id=1, source_target_pairs={{0,4},{2,6},{4,0},{6,2},{8,12},{10,14},{12,8},{14,10},{16,20},{18,... | collective-permute-start | bytes 589832 | tf_op jit(solution)/shard_map/ppermute | solution.py:651
  41.7 6.0 %collective-permute-start.3 = (bf16[128,768]{1,0:T(8,128)(2,1)}, bf16[128,768]{1,0:T(8,128)(2,1)}, u32[]{:S(2)}, u32[]{:S(2)}) collective-permute-start(bf16[128,768]{1,0:T(8,128)(2,1)} %pad_maximum_fusion.4), channel_id=1, source_target_pairs={{0,8},{2,10},{4,12},{6,14},{8,0},{10,2},{12,4},{14,6},{16,24},{18,... | collective-permute-start | bytes 589832 | tf_op jit(solution)/shard_map/ppermute | solution.py:651
  52.0 9.8 %collective-permute-start.4 = (bf16[128,768]{1,0:T(8,128)(2,1)}, bf16[128,768]{1,0:T(8,128)(2,1)}, u32[]{:S(2)}, u32[]{:S(2)}) collective-permute-start(bf16[128,768]{1,0:T(8,128)(2,1)} %pad_maximum_fusion.5), channel_id=1, source_target_pairs={{0,16},{2,18},{4,20},{6,22},{8,24},{10,26},{12,28},{14,30},{16,0},... | collective-permute-start | bytes 589832 | tf_op jit(solution)/shard_map/ppermute | solution.py:651
  63.8 17.8 %copy-start.8 = (bf16[512,1024]{1,0:T(8,128)(2,1)S(1)}, bf16[512,1024]{1,0:T(8,128)(2,1)}, u32[]{:S(2)}) copy-start(bf16[512,1024]{1,0:T(8,128)(2,1)} %param.33) | copy-start | bytes 3145732
  63.8 21.3 %copy-start.6 = (bf16[512,1024]{1,0:T(8,128)(2,1)S(1)}, bf16[512,1024]{1,0:T(8,128)(2,1)}, u32[]{:S(2)}) copy-start(bf16[512,1024]{1,0:T(8,128)(2,1)} %own_ref.1) | copy-start | bytes 3145732
  81.5 3.6 collective-permute-start.5
  81.6 6.0 %collective-permute-start.8 = (bf16[512,1024]{1,0:T(8,128)(2,1)S(1)}, bf16[512,1024]{1,0:T(8,128)(2,1)S(1)}, u32[]{:S(2)}, u32[]{:S(2)}) collective-permute-start(bf16[512,1024]{1,0:T(8,128)(2,1)S(1)} %copy-done.8), channel_id=1, source_target_pairs={{0,1},{1,0},{2,3},{3,2},{4,5},{5,4},{6,7},{7,6},{8,9},{9,8},{10,11... | collective-permute-start | bytes 3145736 | tf_op jit(solution)/shard_map/ppermute | solution.py:641
  85.1 1.9 copy-start.25
  87.0 36.0 %copy-start.2 = (f32[512,1024]{1,0:T(8,128)}, f32[512,1024]{1,0:T(8,128)S(1)}, u32[]{:S(2)}) copy-start(f32[512,1024]{1,0:T(8,128)S(1)} %get-tuple-element.117) | copy-start | bytes 6291460
  87.3 9.5 %copy-start.14 = (bf16[512,1024]{1,0:T(8,128)(2,1)}, bf16[512,1024]{1,0:T(8,128)(2,1)S(1)}, u32[]{:S(2)}) copy-start(bf16[512,1024]{1,0:T(8,128)(2,1)S(1)} %multiply_convert_fusion.3) | copy-start | bytes 3145732
  87.3 3.4 copy-start.29
  87.3 2.7 collective-permute-start.6
  87.7 15.2 %copy-start.24 = (bf16[1024,1024]{1,0:T(8,128)(2,1)}, bf16[1024,1024]{1,0:T(8,128)(2,1)S(1)}, u32[]{:S(2)}) copy-start(bf16[1024,1024]{1,0:T(8,128)(2,1)S(1)} %constant_dynamic-update-slice_fusion.b_ref) | copy-start | bytes 6291460
  87.7 9.1 %copy-start.30 = (bf16[1024,1408]{1,0:T(8,128)(2,1)S(1)}, bf16[1024,1408]{1,0:T(8,128)(2,1)}, u32[]{:S(2)}) copy-start(bf16[1024,1408]{1,0:T(8,128)(2,1)} %param.30) | copy-start | bytes 8650756
  90.7 6.1 %copy-start.22 = (bf16[512,1024]{1,0:T(8,128)(2,1)}, bf16[512,1024]{1,0:T(8,128)(2,1)S(1)}, u32[]{:S(2)}) copy-start(bf16[512,1024]{1,0:T(8,128)(2,1)S(1)} %collective-permute-done.6) | copy-start | bytes 3145732
  112.2 3.5 copy-start.18
  112.2 3.5 copy-start.16
  119.4 5.6 %copy-start.9 = (bf16[1024,1024]{1,0:T(8,128)(2,1)}, bf16[1024,1024]{1,0:T(8,128)(2,1)S(1)}, u32[]{:S(2)}) copy-start(bf16[1024,1024]{1,0:T(8,128)(2,1)S(1)} %add_convert_fusion) | copy-start | bytes 6291460
  119.5 2.7 collective-permute-start.9
  122.2 1.0 copy-start.4
  125.0 3.0 collective-permute-start.10
  145.4 7.0 %collective-permute-start.11 = (bf16[128,768]{1,0:T(8,128)(2,1)S(1)}, bf16[128,768]{1,0:T(8,128)(2,1)S(1)}, u32[]{:S(2)}, u32[]{:S(2)}) collective-permute-start(bf16[128,768]{1,0:T(8,128)(2,1)S(1)} %pad_maximum_fusion.6), channel_id=1, source_target_pairs={{0,2},{2,0},{4,6},{6,4},{8,10},{10,8},{12,14},{14,12},{16,18},{18,... | collective-permute-start | bytes 589832 | tf_op jit(solution)/shard_map/ppermute | solution.py:651
  154.5 6.9 %collective-permute-start.12 = (bf16[128,768]{1,0:T(8,128)(2,1)S(1)}, bf16[128,768]{1,0:T(8,128)(2,1)S(1)}, u32[]{:S(2)}, u32[]{:S(2)}) collective-permute-start(bf16[128,768]{1,0:T(8,128)(2,1)S(1)} %pad_maximum_fusion.7), channel_id=1, source_target_pairs={{0,4},{2,6},{4,0},{6,2},{8,12},{10,14},{12,8},{14,10},{16,20},{18,... | collective-permute-start | bytes 589832 | tf_op jit(solution)/shard_map/ppermute | solution.py:651
  155.7 5.9 %copy-start.13 = (f32[128,512]{1,0:T(8,128)S(1)}, f32[128,512]{1,0:T(8,128)}, u32[]{:S(2)}) copy-start(f32[128,512]{1,0:T(8,128)} %get-tuple-element.71) | copy-start | bytes 786436
  155.7 6.8 %copy-start.17 = (bf16[1024,1408]{1,0:T(8,128)(2,1)S(1)}, bf16[1024,1408]{1,0:T(8,128)(2,1)}, u32[]{:S(2)}) copy-start(bf16[1024,1408]{1,0:T(8,128)(2,1)} %copy-done.16) | copy-start | bytes 8650756
  155.7 6.8 %copy-start.19 = (bf16[1024,1408]{1,0:T(8,128)(2,1)S(1)}, bf16[1024,1408]{1,0:T(8,128)(2,1)}, u32[]{:S(2)}) copy-start(bf16[1024,1408]{1,0:T(8,128)(2,1)} %copy-done.18) | copy-start | bytes 8650756
  161.3 15.9 %copy-start.20 = (bf16[1024,1024]{1,0:T(8,128)(2,1)}, bf16[1024,1024]{1,0:T(8,128)(2,1)S(1)}, u32[]{:S(2)}) copy-start(bf16[1024,1024]{1,0:T(8,128)(2,1)S(1)} %convolution_convert_fusion) | copy-start | bytes 6291460
  161.8 5.9 %collective-permute-start.13 = (bf16[128,768]{1,0:T(8,128)(2,1)S(1)}, bf16[128,768]{1,0:T(8,128)(2,1)S(1)}, u32[]{:S(2)}, u32[]{:S(2)}) collective-permute-start(bf16[128,768]{1,0:T(8,128)(2,1)S(1)} %pad_maximum_fusion.8), channel_id=1, source_target_pairs={{0,8},{2,10},{4,12},{6,14},{8,0},{10,2},{12,4},{14,6},{16,24},{18,... | collective-permute-start | bytes 589832 | tf_op jit(solution)/shard_map/ppermute | solution.py:651
  168.2 10.2 %collective-permute-start.14 = (bf16[128,768]{1,0:T(8,128)(2,1)S(1)}, bf16[128,768]{1,0:T(8,128)(2,1)S(1)}, u32[]{:S(2)}, u32[]{:S(2)}) collective-permute-start(bf16[128,768]{1,0:T(8,128)(2,1)S(1)} %pad_maximum_fusion.9), channel_id=1, source_target_pairs={{0,16},{2,18},{4,20},{6,22},{8,24},{10,26},{12,28},{14,30},{16,0},... | collective-permute-start | bytes 589832 | tf_op jit(solution)/shard_map/ppermute | solution.py:651
  177.2 1.2 copy-start.21
  178.2 270.8 %collective-permute-start.7 = (bf16[512,1024]{1,0:T(8,128)(2,1)}, bf16[512,1024]{1,0:T(8,128)(2,1)}, u32[]{:S(2)}, u32[]{:S(2)}) collective-permute-start(bf16[512,1024]{1,0:T(8,128)(2,1)} %slice.223), channel_id=1, source_target_pairs={{0,1},{1,0},{2,3},{3,2},{4,5},{5,4},{6,7},{7,6},{8,9},{9,8},{10,11... | collective-permute-start | bytes 3145736 | tf_op jit(solution)/shard_map/ppermute | solution.py:641
  179.8 23.5 %copy-start.15 = (bf16[512,1024]{1,0:T(8,128)(2,1)S(1)}, bf16[512,1024]{1,0:T(8,128)(2,1)}, u32[]{:S(2)}) copy-start(bf16[512,1024]{1,0:T(8,128)(2,1)} %copy-done.14) | copy-start | bytes 3145732
  179.8 23.5 %copy-start.23 = (bf16[512,1024]{1,0:T(8,128)(2,1)S(1)}, bf16[512,1024]{1,0:T(8,128)(2,1)}, u32[]{:S(2)}) copy-start(bf16[512,1024]{1,0:T(8,128)(2,1)} %copy-done.22) | copy-start | bytes 3145732
  202.7 25.8 %collective-permute-start.15 = (bf16[512,1024]{1,0:T(8,128)(2,1)}, bf16[512,1024]{1,0:T(8,128)(2,1)S(1)}, u32[]{:S(2)}, u32[]{:S(2)}) collective-permute-start(bf16[512,1024]{1,0:T(8,128)(2,1)} %get-tuple-element.74), channel_id=1, source_target_pairs={{0,1},{1,0},{2,3},{3,2},{4,5},{5,4},{6,7},{7,6},{8,9},{9,8},{10,11... | collective-permute-start | bytes 3145736 | tf_op jit(solution)/shard_map/ppermute | solution.py:641
  219.9 8.6 %copy-start.7 = (bf16[512,1024]{1,0:T(8,128)(2,1)S(1)}, bf16[512,1024]{1,0:T(8,128)(2,1)}, u32[]{:S(2)}) copy-start(bf16[512,1024]{1,0:T(8,128)(2,1)} %own_ref.1) | copy-start | bytes 3145732
  219.9 8.6 %copy-start.11 = (bf16[512,1024]{1,0:T(8,128)(2,1)S(1)}, bf16[512,1024]{1,0:T(8,128)(2,1)}, u32[]{:S(2)}) copy-start(bf16[512,1024]{1,0:T(8,128)(2,1)} %get-tuple-element.73) | copy-start | bytes 3145732
  219.9 8.6 %copy-start.26 = (f32[1024]{0:T(1024)S(1)}, f32[1024]{0:T(1024)}, u32[]{:S(2)}) copy-start(f32[1024]{0:T(1024)} %param.20) | copy-start | bytes 12292
  228.5 0.9 copy-start.27
  228.5 0.9 copy-start.28
  228.5 1.5 copy-start.12
  230.0 219.0 %copy-start.3 = (f32[512,1024]{1,0:T(8,128)S(1)}, f32[512,1024]{1,0:T(8,128)}, u32[]{:S(2)}) copy-start(f32[512,1024]{1,0:T(8,128)} %copy-done.2) | copy-start | bytes 6291460
  230.0 219.0 %copy-start.5 = (bf16[512,1024]{1,0:T(8,128)(2,1)S(1)}, bf16[512,1024]{1,0:T(8,128)(2,1)}, u32[]{:S(2)}) copy-start(bf16[512,1024]{1,0:T(8,128)(2,1)} %copy-done.4) | copy-start | bytes 3145732
  447.7 29.1 %collective-permute-start.16 = (f32[2,1024]{1,0:T(2,128)S(1)}, f32[2,1024]{1,0:T(2,128)S(1)}, u32[]{:S(2)}, u32[]{:S(2)}) collective-permute-start(f32[2,1024]{1,0:T(2,128)S(1)} %reshape.129), channel_id=1, source_target_pairs={{0,1},{1,0},{2,3},{3,2},{4,5},{5,4},{6,7},{7,6},{8,9},{9,8},{10,11... | collective-permute-start | bytes 24584 | tf_op jit(solution)/shard_map/ppermute | solution.py:641
  468.1 9.4 %copy-start.1 = (bf16[1408,1024]{1,0:T(8,128)(2,1)S(1)}, bf16[1408,1024]{1,0:T(8,128)(2,1)}, u32[]{:S(2)}) copy-start(bf16[1408,1024]{1,0:T(8,128)(2,1)} %param.31) | copy-start | bytes 8650756
